TPU v7x, 256 devices: a whole 4x4x8 slice. The times are simulated.
256 devices in a mesh: gx: 32 (over z, x), ta: 8 (over y, core).
Axes of the slice: x: 4, y: 4, z: 8, core: 2. Of those that a mesh axis runs over, the one named last changes fastest.
Arguments:
- field: bfloat16 [1024, 8, 57344], P('ta', None, 'gx')
- weight: float32 [57344], P('gx'), may hold values from 0.2 to 2
- coef: float32 [5, 224], replicated, may hold values from -1 to 1
- window_start: int32 [32], replicated, may hold values from 0 to 247, as said below
- window_end: int32 [32], replicated, may hold values from 16 to 256, as said below
- owner_map: int32 [32], replicated, may hold values from 0 to 31, each once
Outputs:
- owned_gram: float32 [32, 1024, 1024], P('gx', 'ta')
Inputs may be any that keep to these rules, and one draw needn't show every extreme that they name: `window_start`: window w starts 1 to 8 stations before w * 8, the first window at 0; some window starts exactly 8 stations before its block, and the last window starts one station before its block. `window_end`: window w ends 1 to 8 stations after (w + 1) * 8, the last window at 256; some window ends exactly 8 stations after its block. `owner_map`: each gx index owns exactly one window.
All inputs are finite; a program needn't handle non-finite values.
Results may differ from a plain program's by a relative error of at most 0.00077.
Values may be sent and summed in bfloat16 or wider, within the bound.
A program may use at most 64 MiB of HBM per device.

v0:
```python
import jax
import jax.numpy as jnp
from jax import lax
from jax.sharding import PartitionSpec as P

SPAN = 8
NYW = 224
BAND = 2


def padded_2(block, sides, width):
    for axis, dim in sides:
        count = lax.axis_size(axis)
        forward = [(i, i + 1) for i in range(count - 1)]
        backward = [(target, source) for source, target in forward]
        low = lax.ppermute(
            lax.slice_in_dim(block, block.shape[dim] - width, None, axis=dim), axis, forward
        )
        high = lax.ppermute(lax.slice_in_dim(block, 0, width, axis=dim), axis, backward)
        block = jnp.concatenate([low, block, high], axis=dim)
    return block


def station_mask(begin, count, lower, upper):
    stations = begin + jnp.arange(count, dtype=jnp.int32)
    inside = (stations >= lower) & (stations < upper)
    return jnp.repeat(inside, NYW).astype(jnp.bfloat16)


def on_device(field, weight, coef, window_start, window_end, owner_map):
    lines = lax.all_to_all(field, "ta", split_axis=1, concat_axis=0, tiled=True)
    total = lines.shape[0]
    span_local = lines.shape[1]
    width = lines.shape[2]
    stations = width // NYW
    values = lines.astype(jnp.float32)
    centered = values - jnp.mean(values, axis=0, keepdims=True)
    shaped = centered.reshape(total, span_local, stations, NYW)
    padded = jnp.pad(shaped, ((0, 0), (0, 0), (0, 0), (BAND, BAND)))
    filtered = jnp.zeros(shaped.shape, jnp.float32)
    for offset in range(2 * BAND + 1):
        filtered = filtered + coef[offset] * padded[..., offset : offset + NYW]
    factor = jnp.sqrt(weight).reshape(stations, NYW)
    scaled = (filtered * factor).astype(jnp.bfloat16).reshape(total, span_local, width)
    place = lax.axis_index("gx")
    first = window_start[place]
    last = window_end[place]
    wide = padded_2(scaled, (("gx", 2),), width)
    mask = station_mask((place - 1) * stations, 3 * stations, first, last)
    partial_value = jnp.einsum("tsf,usf->tu", wide * mask, wide, preferred_element_type=jnp.float32)
    rows = lax.psum_scatter(partial_value, "ta", scatter_dimension=0, tiled=True)
    gram = rows / ((last - first) * SPAN * NYW).astype(jnp.float32)
    chosen = (owner_map == place).astype(jnp.float32)
    owned = jnp.sum(
        chosen[:, None, None] * lax.all_gather(gram[None], "gx", axis=0, tiled=True), axis=0
    )
    return owned[None]


def solution(mesh):
    placed = (P("ta", None, "gx"), P("gx"), P(), P(), P(), P())
    return jax.shard_map(
        on_device, mesh=mesh, in_specs=placed, out_specs=P("gx", "ta", None), check_vma=False
    )
```

profile of v0, /device:TPU:2, one launch (start us, length us, event | category | flops | bytes accessed | tf_op | source)
XLA Modules:
  0.0 445.1 jit_solution(16185326591842972981)
XLA Ops:
  6.5 6.3 %copy.8 = bf16[128,8,1792]{0,2,1:T(8,128)(2,1)} copy(bf16[128,8,1792]{2,1,0:T(8,128)(2,1)} %param.6) | data formatting | bytes 7340032 | tf_op args[0]
  12.8 4.5 %all-to-all-start = ((bf16[128,8,1792]{0,2,1:T(8,128)(2,1)}), bf16[128,8,1792]{0,2,1:T(8,128)(2,1)}, u32[]{:S(2)}, u32[]{:S(2)}) async-start(bf16[128,8,1792]{0,2,1:T(8,128)(2,1)} %copy.8), calls=%async_computation | async-start | bytes 7340032 | tf_op jit(solution)/shard_map/all_to_all | solution.py:31
  17.4 0.1 mul.125
  17.5 44.0 %all-to-all-done = bf16[128,8,1792]{0,2,1:T(8,128)(2,1)} async-done(((bf16[128,8,1792]{0,2,1:T(8,128)(2,1)}), bf16[128,8,1792]{0,2,1:T(8,128)(2,1)}, u32[]{:S(2)}, u32[]{:S(2)}) %all-to-all-start) | async-done | bytes 3670048 | tf_op jit(solution)/shard_map/all_to_all | solution.py:31
  61.5 14.9 %fusion.13 = f32[1792]{0:T(1024)S(1)} fusion(bf16[128,8,1792]{0,2,1:T(8,128)(2,1)} %all-to-all-done), kind=kLoop, calls=%fused_computation.19 | loop fusion | flops 3668224 | bytes 3677184 | tf_op jit(solution)/shard_map/reduce_sum | solution.py:37
  76.4 0.1 div.16
  76.5 11.1 %copy_convert_fusion = f32[128,8,1792]{0,1,2:T(8,128)S(1)} fusion(bf16[128,8,1792]{0,2,1:T(8,128)(2,1)} %all-to-all-done), kind=kLoop, calls=%fused_computation.17 | loop fusion | flops 1835008 | bytes 11010048 | tf_op jit(solution)/shard_map/convert_element_type | solution.py:36
  87.6 6.4 %broadcast_subtract_fusion = f32[1024,1,8,224]{0,1,3,2:T(1,128)S(1)} fusion(f32[1024,1,8,224]{0,1,3,2:T(1,128)S(1)} %bitcast.24, f32[8,224]{1,0:T(8,128)S(1)} %div.16), kind=kLoop, calls=%fused_computation.18 | loop fusion | flops 1835008 | bytes 14687232 | tf_op jit(solution)/shard_map/sub | solution.py:37
  94.0 29.6 %multiply_convert_fusion = bf16[1024,1,8,224]{0,1,3,2:T(2,128)(2,1)S(1)} fusion(f32[1024,1,8,224]{0,1,3,2:T(1,128)S(1)} %broadcast_subtract_fusion, f32[224]{0:T(256)S(1)} %bitcast.29, f32[224]{0:T(256)S(1)} %bitcast.30, f32[224]{0:T(256)S(1)} %bitcast.27, f32[224]{0:T(256)S(1)} %bitcast.28, f32[224]{0:T(256)S(1)} %bitcast.26, f32[8,224]{1,0:T(8,128)S(1)} %mul.125), kind=kLoop, calls=%fused_computation.13 | loop fusion | flops 20185088 | bytes 11021696 | tf_op jit(solution)/shard_map/convert_element_type | solution.py:44
  123.6 3.3 copy.10
  126.9 4.1 collective-permute-start.1
  130.9 1.9 collective-permute-start
  132.9 0.6 dynamic_slice.7
  133.5 0.6 dynamic_slice.6
  134.0 1.2 and_convert_fusion
  135.3 0.1 broadcast_in_dim.12
  135.3 0.1 convert_element_type.62
  135.4 74.5 %collective-permute-done.1 = bf16[1024,1,1792]{0,2,1:T(8,128)(2,1)} collective-permute-done((bf16[1024,1,1792]{0,2,1:T(8,128)(2,1)}, bf16[1024,1,1792]{0,2,1:T(8,128)(2,1)}, u32[]{:S(2)}, u32[]{:S(2)}) %collective-permute-start.1) | collective-permute-done | bytes 3670048 | tf_op jit(solution)/shard_map/ppermute | solution.py:19
  209.9 3.8 collective-permute-done
  213.8 32.2 %fusion.1 = f32[1024,1024]{1,0:T(8,128)} fusion(bf16[1024,1,1,1,1,1,1792]{0,6,5,4,3,2,1:T(8,128)(2,1)} %bitcast.9, bf16[1024,1,1,1,1,1,1792]{0,6,5,4,3,2,1:T(8,128)(2,1)} %bitcast.19, bf16[1024,1,1,1,1,1,1792]{0,6,5,4,3,2,1:T(8,128)(2,1)} %bitcast.8, bf16[1024,1,1792]{0,2,1:T(8,128)(2,1)} %collective-permute-done.1, bf16[1024,1,1792]{0,2,1:T(8,128)(2,1)} %bitcast.18, ...), kind=kOutput, calls=%fused_computation.3 | convolution fusion | flops 11351359488 | bytes 26225152 | tf_op jit(solution)/shard_map/tsf,usf->tu/dot_general | solution.py:50
  247.2 41.2 %reduce-scatter.2.cloned.1.call-done = f32[128,1024]{1,0:T(8,128)} async-done(((f32[1024,1024]{1,0:T(8,128)}), f32[128,1024]{1,0:T(8,128)}) %reduce-scatter.2.cloned.1.call-update) | async-done | bytes 524304 | tf_op jit(solution)/shard_map/reduce_scatter | solution.py:51
  288.4 1.9 broadcast_divide_fusion
  290.4 138.9 %all-gather.3.cloned.1.call-done = f32[4096,1024]{1,0:T(8,128)} async-done(((f32[128,1024]{1,0:T(8,128)}), f32[4096,1024]{1,0:T(8,128)}) %all-gather.3.cloned.1.call-update) | async-done | bytes 16777232 | tf_op jit(solution)/shard_map/all_gather | solution.py:55
  429.2 9.0 %multiply_reduce_fusion = f32[128,1024]{1,0:T(8,128)} fusion(f32[32,128,1024]{2,1,0:T(8,128)} %bitcast.25, f32[32]{0:T(128)S(1)} %compare_convert_fusion), kind=kLoop, calls=%fused_computation | loop fusion | flops 8257536 | bytes 17301632 | tf_op jit(solution)/shard_map/reduce_sum | solution.py:54
  (18 shorter events, 0.2 us)
Async XLA Ops:
  6.5 10.8 %copy-start = (f32[1792]{0:T(1024)S(1)}, f32[1792]{0:T(1024)}, u32[]{:S(2)}) copy-start(f32[1792]{0:T(1024)} %param.7) | copy-start | bytes 21508
  6.5 10.9 %copy-start.1 = (f32[5,224]{1,0:T(8,128)S(1)}, f32[5,224]{1,0:T(8,128)}, u32[]{:S(2)}) copy-start(f32[5,224]{1,0:T(8,128)} %param.8) | copy-start | bytes 13444
  12.8 48.6 %all-to-all-start = ((bf16[128,8,1792]{0,2,1:T(8,128)(2,1)}), bf16[128,8,1792]{0,2,1:T(8,128)(2,1)}, u32[]{:S(2)}, u32[]{:S(2)}) async-start(bf16[128,8,1792]{0,2,1:T(8,128)(2,1)} %copy.8), calls=%async_computation | async-start | bytes 7340032 | tf_op jit(solution)/shard_map/all_to_all | solution.py:31
  17.3 271.1 %reduce-scatter.2.cloned.1.call-start = ((), (), s32[]{:S(2)}) async-start(), calls=%async_computation.2 | async-start | bytes 4718592 | tf_op jit(solution)/shard_map/reduce_scatter | solution.py:51
  123.5 9.3 %copy-start.2 = (s32[32]{0:T(128)S(1)}, s32[32]{0:T(128)}, u32[]{:S(2)}) copy-start(s32[32]{0:T(128)} %param.10) | copy-start | bytes 388
  123.6 9.9 %copy-start.3 = (s32[32]{0:T(128)S(1)}, s32[32]{0:T(128)}, u32[]{:S(2)}) copy-start(s32[32]{0:T(128)} %param.9) | copy-start | bytes 388
  126.9 83.1 %collective-permute-start.1 = (bf16[1024,1,1792]{0,2,1:T(8,128)(2,1)}, bf16[1024,1,1792]{0,2,1:T(8,128)(2,1)}, u32[]{:S(2)}, u32[]{:S(2)}) collective-permute-start(bf16[1024,1,1792]{0,2,1:T(8,128)(2,1)} %bitcast.18), channel_id=1, source_target_pairs={{8,0},{16,8},{24,16},{32,24},{40,32},{48,40},{56,48},{64,56},{72,6... | collective-permute-start | bytes 11010056 | tf_op jit(solution)/shard_map/ppermute | solution.py:19
  130.9 82.8 %collective-permute-start = (bf16[1024,1,1792]{0,2,1:T(8,128)(2,1)}, bf16[1024,1,1792]{0,2,1:T(8,128)(2,1)}, u32[]{:S(2)}, u32[]{:S(2)}) collective-permute-start(bf16[1024,1,1792]{0,2,1:T(8,128)(2,1)} %bitcast.18), channel_id=1, source_target_pairs={{0,8},{8,16},{16,24},{24,32},{32,40},{40,48},{48,56},{56,64},{64,7... | collective-permute-start | bytes 11010056 | tf_op jit(solution)/shard_map/ppermute | solution.py:16
  213.8 76.6 %copy-start.4 = (s32[32]{0:T(128)S(1)}, s32[32]{0:T(128)}, u32[]{:S(2)}) copy-start(s32[32]{0:T(128)} %param.11) | copy-start | bytes 388
  246.0 183.3 %all-gather.3.cloned.1.call-start = ((), (), s32[]{:S(2)}) async-start(), calls=%async_computation.3 | async-start | bytes 17301504 | tf_op jit(solution)/shard_map/all_gather | solution.py:55
Sparse Core Ops, SparseCore 0:
  246.1 42.3 reduce-scatter.1
  291.0 138.1 all-gather.2
where the time goes:
time: 447 us; the launch traced here: 445 us
  waiting for transfers between devices  302 us (68%)
  other arithmetic  74.1 us (17%)
  matrix products  32.2 us (7%)
  between operations  14.8 us (3%)
  local copies, waits for them, and re-layouts  11.1 us (2%)
  starting transfers between devices  10.6 us (2%)
    all_gather x1, waiting for transfers between devices, on_device(): lax.all_gather(gram[None], 'gx', axis=0, tiled=True)  139 us
    ppermute x1, waiting for transfers between devices, padded_2(): lax.ppermute(lax.slice_in_dim(block, 0, width, axis=dim), axis, backward)  74.5 us
    all_to_all x1, waiting for transfers between devices, on_device(): lines = lax.all_to_all(field, 'ta', split_axis=1, concat_axis=0, tiled=True)  44 us
    reduce_scatter x1, waiting for transfers between devices, on_device(): lax.psum_scatter(partial_value, 'ta', scatter_dimension=0, tiled=True)  41.2 us
    dot_general x1, matrix products, on_device(): jnp.einsum('tsf,usf->tu', wide * mask, wide, preferred_element_type=jnp.f...  32.2 us
    convert_element_type x1, other arithmetic, on_device(): (filtered * factor).astype(jnp.bfloat16).reshape(total, span_local, width)  29.6 us
    reduce_sum x1, other arithmetic, on_device(): centered = values - jnp.mean(values, axis=0, keepdims=True)  14.9 us
    convert_element_type x1, other arithmetic, on_device(): values = lines.astype(jnp.float32)  11.1 us
  transfers between devices with their start and end apart: 5, of which 5 were waited for; matrix products, arithmetic and copies ran while one was open for 1% of the time, Pallas kernels for 0%

commit v1 on v0

--- a/solution.py
+++ b/solution.py
@@ -50,10 +50,16 @@
     partial_value = jnp.einsum("tsf,usf->tu", wide * mask, wide, preferred_element_type=jnp.float32)
     rows = lax.psum_scatter(partial_value, "ta", scatter_dimension=0, tiled=True)
     gram = rows / ((last - first) * SPAN * NYW).astype(jnp.float32)
-    chosen = (owner_map == place).astype(jnp.float32)
-    owned = jnp.sum(
-        chosen[:, None, None] * lax.all_gather(gram[None], "gx", axis=0, tiled=True), axis=0
+    groups = lax.axis_size("gx")
+    order = jnp.arange(groups, dtype=jnp.int32)
+    source = jnp.sum(jnp.where(owner_map[None, :] == order[:, None], order[None, :], 0), axis=1)
+    pieces = gram.reshape(groups, gram.shape[0] // groups, gram.shape[1])
+    spread = lax.all_to_all(pieces, "gx", split_axis=0, concat_axis=0, tiled=True)
+    sorted_pieces = jnp.concatenate(
+        [lax.dynamic_slice_in_dim(spread, source[d], 1, axis=0) for d in range(groups)], axis=0
     )
+    owned = lax.all_to_all(sorted_pieces, "gx", split_axis=0, concat_axis=0, tiled=True)
+    owned = owned.reshape(gram.shape)
     return owned[None]
 
 

time: 447 us -> 397 us (0.89)
  waiting for transfers between devices: 302 us -> 162 us
  between operations: 14.8 us -> 75.2 us
  blocking collectives: 0 us -> 22.9 us
  starting transfers between devices: 10.6 us -> 22.4 us
  other arithmetic: 74.1 us -> 64.5 us
    all_gather x1 -> x0, waiting for transfers between devices: 139 us -> none  [on_device(): lax.all_gather(gram[None], 'gx', axis=0, tiled=True)]
    ppermute x1, waiting for transfers between devices: 74.5 us -> 3.13 us  [padded_2(): lax.ppermute(lax.slice_in_dim(block, 0, width, axis=dim), axis, backward)]
    ppermute x1, waiting for transfers between devices: 3.82 us -> 72.7 us  [padded_2(): lax.ppermute(lax.slice_in_dim(block, block.shape[dim] - width, None, axis...]
    all_to_all x0 -> x1, blocking collectives: none -> 22.9 us  [on_device(): lax.all_to_all(sorted_pieces, 'gx', split_axis=0, concat_axis=0, tiled=True)]
    all_to_all x0 -> x1, starting transfers between devices: none -> 10.1 us  [on_device(): lax.all_to_all(pieces, 'gx', split_axis=0, concat_axis=0, tiled=True)]
    reduce_sum x1, other arithmetic: 9.04 us -> 0.11 us  [on_device(): jnp.sum(jnp.where(owner_map[None, :] == order[:, None], order[None, :], 0...]
    unnamed x12 -> x43, local copies, waits for them, and re-layouts: 9.59 us -> 10.1 us
  transfers between devices with their start and end apart: 5 -> 5, of which waited for: 5 -> 4; matrix products, arithmetic and copies ran while one was open for 1% -> 1% of each run, Pallas kernels for 0% -> 0%
where the time goes in v1:
time: 397 us; the launch traced here: 394 us
  waiting for transfers between devices  162 us (41%)
  between operations  75.2 us (19%)
  other arithmetic  64.5 us (16%)
  matrix products  32.2 us (8%)
  blocking collectives  22.9 us (6%)
  starting transfers between devices  22.4 us (6%)
  local copies, waits for them, and re-layouts  15 us (4%)
    ppermute x1, waiting for transfers between devices, padded_2(): lax.ppermute(lax.slice_in_dim(block, block.shape[dim] - width, None, axis...  72.7 us
    all_to_all x1, waiting for transfers between devices, on_device(): lines = lax.all_to_all(field, 'ta', split_axis=1, concat_axis=0, tiled=True)  44 us
    reduce_scatter x1, waiting for transfers between devices, on_device(): lax.psum_scatter(partial_value, 'ta', scatter_dimension=0, tiled=True)  42.2 us
    dot_general x1, matrix products, on_device(): jnp.einsum('tsf,usf->tu', wide * mask, wide, preferred_element_type=jnp.f...  32.2 us
    convert_element_type x1, other arithmetic, on_device(): (filtered * factor).astype(jnp.bfloat16).reshape(total, span_local, width)  29.6 us
    all_to_all x1, blocking collectives, on_device(): lax.all_to_all(sorted_pieces, 'gx', split_axis=0, concat_axis=0, tiled=True)  22.9 us
    reduce_sum x1, other arithmetic, on_device(): centered = values - jnp.mean(values, axis=0, keepdims=True)  14.9 us
    convert_element_type x1, other arithmetic, on_device(): values = lines.astype(jnp.float32)  11.1 us
  transfers between devices with their start and end apart: 5, of which 4 were waited for; matrix products, arithmetic and copies ran while one was open for 1% of the time, Pallas kernels for 0%

profile of v1, /device:TPU:2, one launch (start us, length us, event | category | flops | bytes accessed | tf_op | source)
XLA Modules:
  0.0 394.1 jit_solution(2725819887126767632)
XLA Ops:
  6.5 6.3 %copy.10 = bf16[128,8,1792]{0,2,1:T(8,128)(2,1)} copy(bf16[128,8,1792]{2,1,0:T(8,128)(2,1)} %param.6) | data formatting | bytes 7340032 | tf_op args[0]
  12.8 4.5 %all-to-all-start = ((bf16[128,8,1792]{0,2,1:T(8,128)(2,1)}), bf16[128,8,1792]{0,2,1:T(8,128)(2,1)}, u32[]{:S(2)}, u32[]{:S(2)}) async-start(bf16[128,8,1792]{0,2,1:T(8,128)(2,1)} %copy.10), calls=%async_computation | async-start | bytes 7340032 | tf_op jit(solution)/shard_map/all_to_all | solution.py:31
  17.5 44.0 %all-to-all-done = bf16[128,8,1792]{0,2,1:T(8,128)(2,1)} async-done(((bf16[128,8,1792]{0,2,1:T(8,128)(2,1)}), bf16[128,8,1792]{0,2,1:T(8,128)(2,1)}, u32[]{:S(2)}, u32[]{:S(2)}) %all-to-all-start) | async-done | bytes 3670048 | tf_op jit(solution)/shard_map/all_to_all | solution.py:31
  61.5 14.9 %fusion.13 = f32[1792]{0:T(1024)S(1)} fusion(bf16[128,8,1792]{0,2,1:T(8,128)(2,1)} %all-to-all-done), kind=kLoop, calls=%fused_computation.18 | loop fusion | flops 3668224 | bytes 3677184 | tf_op jit(solution)/shard_map/reduce_sum | solution.py:37
  76.5 11.1 %copy_convert_fusion = f32[128,8,1792]{0,1,2:T(8,128)S(1)} fusion(bf16[128,8,1792]{0,2,1:T(8,128)(2,1)} %all-to-all-done), kind=kLoop, calls=%fused_computation.16 | loop fusion | flops 1835008 | bytes 11010048 | tf_op jit(solution)/shard_map/convert_element_type | solution.py:36
  87.6 6.4 %broadcast_subtract_fusion = f32[1024,1,8,224]{0,1,3,2:T(1,128)S(1)} fusion(f32[1024,1,8,224]{0,1,3,2:T(1,128)S(1)} %bitcast.54, f32[8,224]{1,0:T(8,128)S(1)} %div.16), kind=kLoop, calls=%fused_computation.17 | loop fusion | flops 1835008 | bytes 14687232 | tf_op jit(solution)/shard_map/sub | solution.py:37
  94.0 29.6 %multiply_convert_fusion = bf16[1024,1,8,224]{0,1,3,2:T(2,128)(2,1)S(1)} fusion(f32[1024,1,8,224]{0,1,3,2:T(1,128)S(1)} %broadcast_subtract_fusion, f32[224]{0:T(256)S(1)} %bitcast.58, f32[224]{0:T(256)S(1)} %bitcast.59, f32[224]{0:T(256)S(1)} %bitcast.56, f32[224]{0:T(256)S(1)} %bitcast.57, f32[224]{0:T(256)S(1)} %bitcast.55, f32[8,224]{1,0:T(8,128)S(1)} %mul.116), kind=kLoop, calls=%fused_computation.12 | loop fusion | flops 20185088 | bytes 11021696 | tf_op jit(solution)/shard_map/convert_element_type | solution.py:44
  123.6 3.3 copy.12
  126.9 3.4 collective-permute-start
  130.3 4.3 %collective-permute-start.1 = (bf16[1024,1,1792]{0,2,1:T(8,128)(2,1)}, bf16[1024,1,1792]{0,2,1:T(8,128)(2,1)}, u32[]{:S(2)}, u32[]{:S(2)}) collective-permute-start(bf16[1024,1,1792]{0,2,1:T(8,128)(2,1)} %bitcast.48), channel_id=1, source_target_pairs={{8,0},{16,8},{24,16},{32,24},{40,32},{48,40},{56,48},{64,56},{72,6... | collective-permute-start | bytes 11010056 | tf_op jit(solution)/shard_map/ppermute | solution.py:19
  134.6 0.6 dynamic_slice.102
  135.2 0.6 dynamic_slice.103
  135.8 1.3 and_convert_fusion
  137.3 72.7 %collective-permute-done = bf16[1024,1,1792]{0,2,1:T(8,128)(2,1)} collective-permute-done((bf16[1024,1,1792]{0,2,1:T(8,128)(2,1)}, bf16[1024,1,1792]{0,2,1:T(8,128)(2,1)}, u32[]{:S(2)}, u32[]{:S(2)}) %collective-permute-start) | collective-permute-done | bytes 3670048 | tf_op jit(solution)/shard_map/ppermute | solution.py:16
  209.9 3.1 collective-permute-done.1
  213.1 32.2 %fusion.1 = f32[1024,1024]{1,0:T(8,128)} fusion(bf16[1024,1,1,1,1,1,1792]{0,6,5,4,3,2,1:T(8,128)(2,1)} %bitcast.9, bf16[1024,1,1,1,1,1,1792]{0,6,5,4,3,2,1:T(8,128)(2,1)} %bitcast.49, bf16[1024,1,1,1,1,1,1792]{0,6,5,4,3,2,1:T(8,128)(2,1)} %bitcast.8, bf16[1024,1,1792]{0,2,1:T(8,128)(2,1)} %collective-permute-done.1, bf16[1024,1,1792]{0,2,1:T(8,128)(2,1)} %bitcast.48, ...), kind=kOutput, calls=%fused_computation.2 | convolution fusion | flops 11351359488 | bytes 26225152 | tf_op jit(solution)/shard_map/tsf,usf->tu/dot_general | solution.py:50
  246.6 42.2 %reduce-scatter.2.cloned.1.call-done = f32[128,1024]{1,0:T(8,128)} async-done(((f32[1024,1024]{1,0:T(8,128)}), f32[128,1024]{1,0:T(8,128)}) %reduce-scatter.2.cloned.1.call-update) | async-done | bytes 524304 | tf_op jit(solution)/shard_map/reduce_scatter | solution.py:51
  288.8 1.1 broadcast_divide_fusion
  289.9 0.9 reshape.219
  290.8 10.1 %all-to-all-start.1 = ((f32[32,4,1024]{2,1,0:T(4,128)}), f32[32,4,1024]{2,1,0:T(4,128)S(1)}, u32[]{:S(2)}, u32[]{:S(2)}) async-start(f32[32,4,1024]{2,1,0:T(4,128)} %reshape.219), calls=%async_computation.2 | async-start | bytes 1048576 | tf_op jit(solution)/shard_map/all_to_all | solution.py:57
  301.1 0.7 fusion.17
  318.0 0.7 fusion.16
  363.4 22.9 %all_to_all.19 = f32[32,4,1024]{2,1,0:T(4,128)S(1)} all-to-all(f32[32,4,1024]{2,1,0:T(4,128)S(1)} %constant_dynamic-update-slice_fusion), channel_id=1, replica_groups=mesh['gx'=32,'ta'=8] {'gx'}, dimensions={0} | all-to-all | bytes 1048576 | tf_op jit(solution)/shard_map/all_to_all | solution.py:61
  386.3 1.0 broadcast_in_dim_reshape.4
  (53 shorter events, 1.0 us)
Async XLA Ops:
  6.5 10.9 %copy-start = (f32[1792]{0:T(1024)S(1)}, f32[1792]{0:T(1024)}, u32[]{:S(2)}) copy-start(f32[1792]{0:T(1024)} %param.7) | copy-start | bytes 21508
  6.5 11.0 %copy-start.1 = (f32[5,224]{1,0:T(8,128)S(1)}, f32[5,224]{1,0:T(8,128)}, u32[]{:S(2)}) copy-start(f32[5,224]{1,0:T(8,128)} %param.8) | copy-start | bytes 13444
  12.8 48.6 %all-to-all-start = ((bf16[128,8,1792]{0,2,1:T(8,128)(2,1)}), bf16[128,8,1792]{0,2,1:T(8,128)(2,1)}, u32[]{:S(2)}, u32[]{:S(2)}) async-start(bf16[128,8,1792]{0,2,1:T(8,128)(2,1)} %copy.10), calls=%async_computation | async-start | bytes 7340032 | tf_op jit(solution)/shard_map/all_to_all | solution.py:31
  17.3 271.4 %reduce-scatter.2.cloned.1.call-start = ((), (), s32[]{:S(2)}) async-start(), calls=%async_computation.4 | async-start | bytes 4718592 | tf_op jit(solution)/shard_map/reduce_scatter | solution.py:51
  123.6 11.0 %copy-start.2 = (s32[32]{0:T(128)S(1)}, s32[32]{0:T(128)}, u32[]{:S(2)}) copy-start(s32[32]{0:T(128)} %param.9) | copy-start | bytes 388
  123.6 11.7 %copy-start.3 = (s32[32]{0:T(128)S(1)}, s32[32]{0:T(128)}, u32[]{:S(2)}) copy-start(s32[32]{0:T(128)} %param.10) | copy-start | bytes 388
  126.9 83.1 %collective-permute-start = (bf16[1024,1,1792]{0,2,1:T(8,128)(2,1)}, bf16[1024,1,1792]{0,2,1:T(8,128)(2,1)}, u32[]{:S(2)}, u32[]{:S(2)}) collective-permute-start(bf16[1024,1,1792]{0,2,1:T(8,128)(2,1)} %bitcast.48), channel_id=1, source_target_pairs={{0,8},{8,16},{16,24},{24,32},{32,40},{40,48},{48,56},{56,64},{64,7... | collective-permute-start | bytes 11010056 | tf_op jit(solution)/shard_map/ppermute | solution.py:16
  130.3 82.8 %collective-permute-start.1 = (bf16[1024,1,1792]{0,2,1:T(8,128)(2,1)}, bf16[1024,1,1792]{0,2,1:T(8,128)(2,1)}, u32[]{:S(2)}, u32[]{:S(2)}) collective-permute-start(bf16[1024,1,1792]{0,2,1:T(8,128)(2,1)} %bitcast.48), channel_id=1, source_target_pairs={{8,0},{16,8},{24,16},{32,24},{40,32},{48,40},{56,48},{64,56},{72,6... | collective-permute-start | bytes 11010056 | tf_op jit(solution)/shard_map/ppermute | solution.py:19
  245.3 55.7 %copy-start.4 = (s32[32]{0:T(128)S(1)}, s32[32]{0:T(128)}, u32[]{:S(2)}) copy-start(s32[32]{0:T(128)} %param.11) | copy-start | bytes 388
  290.8 71.9 %all-to-all-start.1 = ((f32[32,4,1024]{2,1,0:T(4,128)}), f32[32,4,1024]{2,1,0:T(4,128)S(1)}, u32[]{:S(2)}, u32[]{:S(2)}) async-start(f32[32,4,1024]{2,1,0:T(4,128)} %reshape.219), calls=%async_computation.2 | async-start | bytes 1048576 | tf_op jit(solution)/shard_map/all_to_all | solution.py:57
Sparse Core Ops, SparseCore 0:
  245.4 43.3 reduce-scatter.1

commit v2 on v0

v2 whole, which is shorter than its diff:
```python
import functools

import jax
import jax.numpy as jnp
from jax import lax
from jax.experimental import pallas as pl
from jax.experimental.pallas import tpu as pltpu
from jax.sharding import PartitionSpec as P

SPAN = 8
NYW = 224
BAND = 2
STATIONS = 8
WIDTH = STATIONS * NYW
TA = 8
MESH = pl.DeviceIdType.MESH
CUTS = (0, 384, 896, 1280, 1792)
CHUNKS = len(CUTS) - 1
KEPT = 5
PAIR = 6


def rotated(me, step, count):
    return lax.rem(me + step, count)


def gram_kernel(
    rows, total, x_ref, taps_ref, part_ref, out_ref,
    sums, send, lines, gram, landed,
    sum_send, sum_recv, line_send, line_recv, line_own, gram_send, gram_recv, gram_own,
):
    place = lax.axis_index("gx")
    me = lax.axis_index("ta")
    wide = KEPT * rows

    for span in range(SPAN):
        def add(step, acc):
            start = pl.multiple_of(step * 16, 16)
            tile = x_ref[span, pl.ds(start, 16), :].astype(jnp.float32)
            return acc + tile[:8] + tile[8:]
        acc = lax.fori_loop(0, rows // 16, add, jnp.zeros((8, WIDTH), jnp.float32))
        sums[me, pl.ds(span, 1), :] = jnp.sum(acc, axis=0, keepdims=True)

    barrier = pltpu.get_barrier_semaphore()

    @pl.loop(1, TA)
    def _(step):
        pl.semaphore_signal(
            barrier, inc=1, device_id=(place, rotated(me, step, TA)), device_id_type=MESH
        )
    pl.semaphore_wait(barrier, TA - 1)

    def sum_copy(owner, target):
        return pltpu.make_async_remote_copy(
            src_ref=sums.at[owner], dst_ref=sums.at[owner],
            send_sem=sum_send.at[target], recv_sem=sum_recv.at[owner],
            device_id=(place, target), device_id_type=MESH,
        )

    @pl.loop(1, TA)
    def _(step):
        sum_copy(me, rotated(me, step, TA)).start()

    @pl.loop(1, TA)
    def _(step):
        sum_copy(rotated(me, step, TA), me).wait_recv()

    mean = jnp.sum(sums[...], axis=0) * (1.0 / total)

    def line_copy(chunk, owner, target):
        lanes = slice(CUTS[chunk], CUTS[chunk + 1])
        return pltpu.make_async_remote_copy(
            src_ref=send.at[target, :, lanes],
            dst_ref=lines.at[pl.ds(pl.multiple_of(owner * rows, rows), rows), lanes],
            send_sem=line_send.at[chunk, target], recv_sem=line_recv.at[chunk, owner],
            device_id=(place, target), device_id_type=MESH,
        )

    def own_copy(chunk):
        lanes = slice(CUTS[chunk], CUTS[chunk + 1])
        return pltpu.make_async_copy(
            send.at[me, :, lanes],
            lines.at[pl.ds(pl.multiple_of(me * rows, rows), rows), lanes],
            line_own.at[chunk],
        )

    for chunk in range(CHUNKS):
        for span in (2 * chunk, 2 * chunk + 1):
            level = mean[span : span + 1]

            @pl.loop(0, rows // 16)
            def _(step):
                start = pl.multiple_of(step * 16, 16)
                centered = x_ref[span, pl.ds(start, 16), :].astype(jnp.float32) - level
                filtered = taps_ref[BAND : BAND + 1, :] * centered
                for offset in range(2 * BAND + 1):
                    if offset != BAND:
                        moved = pltpu.roll(centered, (BAND - offset) % WIDTH, 1)
                        filtered = filtered + taps_ref[offset : offset + 1, :] * moved
                scaled = filtered.astype(jnp.bfloat16)
                for station in range(STATIONS):
                    send[station, pl.ds(start, 16), NYW * span : NYW * (span + 1)] = scaled[
                        :, NYW * station : NYW * (station + 1)
                    ]

        @pl.loop(1, TA)
        def _(step):
            line_copy(chunk, me, rotated(me, step, TA)).start()
        own_copy(chunk).start()

    def gram_copy(owner, target):
        source = gram.at[
            pl.ds(pl.multiple_of(target * rows, rows), rows),
            pl.ds(pl.multiple_of(lax.rem(target, 2) * rows, rows), wide),
        ]
        return pltpu.make_async_remote_copy(
            src_ref=source, dst_ref=landed.at[owner],
            send_sem=gram_send.at[target], recv_sem=gram_recv.at[owner],
            device_id=(place, target), device_id_type=MESH,
        )

    def gram_local():
        source = gram.at[
            pl.ds(pl.multiple_of(me * rows, rows), rows),
            pl.ds(pl.multiple_of(lax.rem(me, 2) * rows, rows), wide),
        ]
        return pltpu.make_async_copy(source, landed.at[me], gram_own)

    pair = 2 * rows
    for chunk in range(CHUNKS):
        lanes = slice(CUTS[chunk], CUTS[chunk + 1])
        own_copy(chunk).wait()

        @pl.loop(1, TA)
        def _(step):
            line_copy(chunk, rotated(me, step, TA), me).wait_recv()

        @pl.loop(1, TA // 2 + 1)
        def _(step):
            row = lax.rem(me // 2 + step, TA // 2)
            where = pl.ds(pl.multiple_of(row * pair, pair), pair)
            left = lines[where, lanes]
            for block in range(PAIR // 2):
                column = lax.rem(row + block, TA // 2)
                right = lines[pl.ds(pl.multiple_of(column * pair, pair), pair), lanes]
                product = lax.dot_general(
                    left, right, (((1,), (1,)), ((), ())), preferred_element_type=jnp.float32
                )
                at = slice(block * pair, (block + 1) * pair)
                if chunk == 0:
                    gram[where, at] = product
                else:
                    gram[where, at] = gram[where, at] + product
            if chunk == CHUNKS - 1:
                for side in range(2):
                    target = 2 * row + side

                    @pl.when(target != me)
                    def _():
                        gram_copy(me, target).start()

    gram_local().start()
    gram_local().wait()

    @pl.loop(0, rows // 8)
    def _(step):
        at = pl.ds(pl.multiple_of(step * 8, 8), 8)
        tile = landed[me, at, :]
        out_ref[0, at, :] = tile
        out_ref[1, at, :] = tile * part_ref[0, me]
        out_ref[2, at, :] = tile * part_ref[1, me]

    @pl.loop(1, TA)
    def _(count):
        owner = rotated(me, TA - count, TA)
        gram_copy(owner, me).wait_recv()
        upper = part_ref[0, owner]
        lower = part_ref[1, owner]

        @pl.loop(0, rows // 8)
        def _(step):
            at = pl.ds(pl.multiple_of(step * 8, 8), 8)
            tile = landed[owner, at, :]
            out_ref[0, at, :] = out_ref[0, at, :] + tile
            out_ref[1, at, :] = out_ref[1, at, :] + tile * upper
            out_ref[2, at, :] = out_ref[2, at, :] + tile * lower

    @pl.loop(1, TA)
    def _(step):
        target = rotated(me, step, TA)
        sum_copy(me, target).wait_send()
        gram_copy(me, target).wait_send()
        for chunk in range(CHUNKS):
            line_copy(chunk, me, target).wait_send()


def owner_kernel(
    groups, rows, sums_ref, source_ref, count_ref, out_ref,
    beside, pieces, spread, ordered, owned, block, turned,
    side_send, side_recv, out_send, out_recv, back_send, back_recv, turn_send, turn_recv, own_sem,
):
    place = lax.axis_index("gx")
    me = lax.axis_index("ta")
    piece = rows // groups
    turns = TA - KEPT

    barrier = pltpu.get_barrier_semaphore()

    @pl.loop(1, groups)
    def _(step):
        pl.semaphore_signal(
            barrier, inc=1, device_id=(rotated(place, step, groups), me), device_id_type=MESH
        )
    for turn in range(1, turns + 1):
        for other in (rotated(me, turn, TA), rotated(me, TA - turn, TA)):
            pl.semaphore_signal(barrier, inc=1, device_id=(place, other), device_id_type=MESH)
    pl.semaphore_wait(barrier, groups - 1 + 2 * turns)

    after = rotated(place, 1, groups)
    before = rotated(place, groups - 1, groups)

    def side_copy(side):
        return pltpu.make_async_remote_copy(
            src_ref=sums_ref.at[1 + side], dst_ref=beside.at[side],
            send_sem=side_send.at[side], recv_sem=side_recv.at[side],
            device_id=((after, before)[side], me), device_id_type=MESH,
        )

    for side in range(2):
        side_copy(side).start()
    for side in range(2):
        side_copy(side).wait()

    @pl.loop(0, rows // 8)
    def _(step):
        at = pl.ds(pl.multiple_of(step * 8, 8), 8)
        tile = (sums_ref[0, at, :] + beside[0, at, :] + beside[1, at, :]) / count_ref[0]
        for part in range(8 // piece):
            pieces[step * (8 // piece) + part] = tile[part * piece : (part + 1) * piece]

    def out_copy(owner, target):
        return pltpu.make_async_remote_copy(
            src_ref=pieces.at[target], dst_ref=spread.at[owner],
            send_sem=out_send.at[target], recv_sem=out_recv.at[owner],
            device_id=(target, me), device_id_type=MESH,
        )

    @pl.loop(1, groups)
    def _(step):
        out_copy(place, rotated(place, step, groups)).start()
    own = pltpu.make_async_copy(pieces.at[place], spread.at[place], own_sem.at[0])
    own.start()
    own.wait()

    @pl.loop(1, groups)
    def _(step):
        out_copy(rotated(place, groups - step, groups), place).wait_recv()

    @pl.loop(0, groups)
    def _(slot):
        ordered[slot] = spread[source_ref[slot]]

    def back_copy(owner, target):
        return pltpu.make_async_remote_copy(
            src_ref=ordered.at[target], dst_ref=owned.at[owner],
            send_sem=back_send.at[target], recv_sem=back_recv.at[owner],
            device_id=(target, me), device_id_type=MESH,
        )

    @pl.loop(1, groups)
    def _(step):
        back_copy(place, rotated(place, step, groups)).start()
    back = pltpu.make_async_copy(ordered.at[place], owned.at[place], own_sem.at[1])
    back.start()
    back.wait()

    @pl.loop(1, groups)
    def _(step):
        back_copy(rotated(place, groups - step, groups), place).wait_recv()

    @pl.loop(0, rows // 8)
    def _(step):
        at = pl.ds(pl.multiple_of(step * 8, 8), 8)
        for part in range(8 // piece):
            tile = owned[step * (8 // piece) + part]
            for column in range(KEPT):
                block[column, pl.ds(step * 8 + part * piece, piece), :] = tile[
                    :, column * rows : (column + 1) * rows
                ]

    def turn_copy(turn):
        return pltpu.make_async_remote_copy(
            src_ref=block.at[turn], dst_ref=turned.at[turn - 1],
            send_sem=turn_send.at[turn - 1], recv_sem=turn_recv.at[turn - 1],
            device_id=(place, rotated(me, turn, TA)), device_id_type=MESH,
        )

    for turn in range(1, turns + 1):
        turn_copy(turn).start()
    for column in range(KEPT):
        target = rotated(me, column, TA)
        out_ref[:, pl.ds(pl.multiple_of(target * rows, rows), rows)] = block[column]
    for turn in range(1, turns + 1):
        turn_copy(turn).wait()
        target = rotated(me, TA - turn, TA)
        out_ref[:, pl.ds(pl.multiple_of(target * rows, rows), rows)] = turned[turn - 1].T

    @pl.loop(1, groups)
    def _(step):
        target = rotated(place, step, groups)
        out_copy(place, target).wait_send()
        back_copy(place, target).wait_send()


def on_device(field, weight, coef, window_start, window_end, owner_map):
    rows = field.shape[0]
    groups = lax.axis_size("gx")
    piece = rows // groups
    total = rows * TA
    place = lax.axis_index("gx")

    lines = jnp.transpose(field, (1, 0, 2))
    point = jnp.arange(NYW, dtype=jnp.int32)[None, :]
    reach = point + jnp.arange(-BAND, BAND + 1, dtype=jnp.int32)[:, None]
    taps = jnp.where((reach >= 0) & (reach < NYW), coef, 0.0)
    taps = jnp.tile(taps, (1, STATIONS)) * jnp.sqrt(weight)[None, :]

    station = place * STATIONS + jnp.arange(STATIONS, dtype=jnp.int32)
    next_start = jnp.where(
        place + 1 < groups, window_start[jnp.minimum(place + 1, groups - 1)], groups * STATIONS
    )
    last_end = jnp.where(place > 0, window_end[jnp.maximum(place - 1, 0)], 0)
    part = jnp.stack([station >= next_start, station < last_end]).astype(jnp.float32)
    count = ((window_end[place] - window_start[place]) * SPAN * NYW).astype(jnp.float32)
    order = jnp.arange(groups, dtype=jnp.int32)
    source = jnp.sum(jnp.where(owner_map[None, :] == order[:, None], order[None, :], 0), axis=1)

    vmem = pl.BlockSpec(memory_space=pltpu.VMEM)
    smem = pl.BlockSpec(memory_space=pltpu.SMEM)
    dma = pltpu.SemaphoreType.DMA
    wide = KEPT * rows
    sums = pl.pallas_call(
        functools.partial(gram_kernel, rows, total),
        out_shape=jax.ShapeDtypeStruct((3, rows, wide), jnp.float32),
        in_specs=[vmem, vmem, smem],
        out_specs=vmem,
        scratch_shapes=[
            pltpu.VMEM((TA, SPAN, WIDTH), jnp.float32),
            pltpu.VMEM((TA, rows, WIDTH), jnp.bfloat16),
            pltpu.VMEM((total, WIDTH), jnp.bfloat16),
            pltpu.VMEM((total, PAIR * rows), jnp.float32),
            pltpu.VMEM((TA, rows, wide), jnp.float32),
            dma((TA,)), dma((TA,)),
            dma((CHUNKS, TA)), dma((CHUNKS, TA)), dma((CHUNKS,)),
            dma((TA,)), dma((TA,)), dma,
        ],
        compiler_params=pltpu.CompilerParams(
            collective_id=0, has_side_effects=True, vmem_limit_bytes=48 * 1024 * 1024
        ),
        name="station_gram",
    )(lines, taps, part)

    turns = TA - KEPT
    owned = pl.pallas_call(
        functools.partial(owner_kernel, groups, rows),
        out_shape=jax.ShapeDtypeStruct((rows, total), jnp.float32),
        in_specs=[vmem, smem, smem],
        out_specs=vmem,
        scratch_shapes=[
            pltpu.VMEM((2, rows, wide), jnp.float32),
            pltpu.VMEM((groups, piece, wide), jnp.float32),
            pltpu.VMEM((groups, piece, wide), jnp.float32),
            pltpu.VMEM((groups, piece, wide), jnp.float32),
            pltpu.VMEM((groups, piece, wide), jnp.float32),
            pltpu.VMEM((KEPT, rows, rows), jnp.float32),
            pltpu.VMEM((turns, rows, rows), jnp.float32),
            dma((2,)), dma((2,)), dma((groups,)), dma((groups,)),
            dma((groups,)), dma((groups,)), dma((turns,)), dma((turns,)), dma((2,)),
        ],
        compiler_params=pltpu.CompilerParams(
            collective_id=1, has_side_effects=True, vmem_limit_bytes=32 * 1024 * 1024
        ),
        name="owner_rows",
    )(sums, source, count[None])
    return owned[None]


def solution(mesh):
    placed = (P("ta", None, "gx"), P("gx"), P(), P(), P(), P())
    return jax.shard_map(
        on_device, mesh=mesh, in_specs=placed, out_specs=P("gx", "ta", None), check_vma=False
    )
```

time: 447 us -> 149 us (0.33)
  waiting for transfers between devices: 302 us -> 0 us
  Pallas kernels: 0 us -> 137 us
  other arithmetic: 74.1 us -> 1.58 us
  matrix products: 32.2 us -> 0 us
  between operations: 14.8 us -> 2.6 us
  starting transfers between devices: 10.6 us -> 0 us
  local copies, waits for them, and re-layouts: 11.1 us -> 5.71 us
    all_gather x1 -> x0, waiting for transfers between devices: 139 us -> none  [on_device(): lax.all_gather(gram[None], 'gx', axis=0, tiled=True)]
    pallas_call x0 -> x2, Pallas kernels: none -> 137 us  [the longest x1 86.4 us: on_device(): pl.pallas_call(functools.partial(gram_kernel, rows, total), out_shape=jax...]
    ppermute x2 -> x0, waiting for transfers between devices: 78.3 us -> none  [the longest x1 74.5 us: padded_2(): lax.ppermute(lax.slice_in_dim(block, 0, width, axis=dim), axis, backward)]
    all_to_all x1 -> x0, waiting for transfers between devices: 44 us -> none  [on_device(): lines = lax.all_to_all(field, 'ta', split_axis=1, concat_axis=0, tiled=True)]
    convert_element_type x4 -> x1, other arithmetic: 41.9 us -> 0.01 us  [on_device(): jnp.stack([station >= next_start, station < last_end]).astype(jnp.float32)]
    reduce_scatter x1 -> x0, waiting for transfers between devices: 41.2 us -> none  [on_device(): lax.psum_scatter(partial_value, 'ta', scatter_dimension=0, tiled=True)]
    dot_general x1 -> x0, matrix products: 32.2 us -> none  [on_device(): jnp.einsum('tsf,usf->tu', wide * mask, wide, preferred_element_type=jnp.f...]
    reduce_sum x2 -> x1, other arithmetic: 24 us -> 0.77 us  [on_device(): jnp.sum(jnp.where(owner_map[None, :] == order[:, None], order[None, :], 0...]
  transfers between devices with their start and end apart: 5 -> 0, of which waited for: 5 -> 0; matrix products, arithmetic and copies ran while one was open for 1% -> 0% of each run, Pallas kernels for 0% -> 0%
where the time goes in v2:
time: 149 us; the launch traced here: 146 us
  Pallas kernels  137 us (92%)
  local copies, waits for them, and re-layouts  5.71 us (4%)
  between operations  2.6 us (2%)
  other arithmetic  1.58 us (1%)
    pallas_call x1, Pallas kernels, on_device(): pl.pallas_call(functools.partial(gram_kernel, rows, total), out_shape=jax...  86.4 us
    pallas_call x1, Pallas kernels, on_device(): pl.pallas_call(functools.partial(owner_kernel, groups, rows), out_shape=j...  50.1 us
    unnamed x2, local copies, waits for them, and re-layouts  3.51 us

profile of v2, /device:TPU:2, one launch (start us, length us, event | category | flops | bytes accessed | tf_op | source)
XLA Modules:
  0.0 146.4 jit_solution(4124452896439304770)
XLA Ops:
  0.0 0.8 select_reduce_fusion.source_ref
  0.8 1.4 fusion.6
  4.8 0.8 fusion.3
  5.5 0.7 sqrt.3
  6.3 0.1 tile.10
  6.4 2.7 %copy.10 = bf16[128,8,1792]{2,0,1:T(8,128)(2,1)S(1)} copy(bf16[128,8,1792]{2,1,0:T(8,128)(2,1)} %param.6) | data formatting | bytes 7340032 | tf_op args[0]
  9.1 86.4 %station_gram.1.sums_ref = f32[3,128,640]{2,1,0:T(8,128)S(1)} custom-call(bf16[8,128,1792]{2,1,0:T(8,128)(2,1)S(1)} %bitcast.6, f32[5,1792]{1,0:T(8,128)S(1)} %broadcast_multiply_fusion.taps_ref, f32[2,8]{1,0:T(2,128)S(1)} %add_convert_fusion.part_ref), custom_call_target="tpu_custom_call" | custom-call | tf_op jit(solution)/shard_map/station_gram/pallas_call | solution.py:342
  95.5 50.1 %owner_rows.1 = f32[128,1024]{1,0:T(8,128)S(1)} custom-call(f32[3,128,640]{2,1,0:T(8,128)S(1)} %station_gram.1.sums_ref, s32[32]{0:T(128)S(1)} %select_reduce_fusion.source_ref, f32[1]{0:T(128)S(6)} %convert_element_type.8.count_ref), custom_call_target="tpu_custom_call" | custom-call | tf_op jit(solution)/shard_map/owner_rows/pallas_call | solution.py:364
  145.6 0.8 copy.12
  (6 shorter events, 0.1 us)

commit v3 on v2

--- a/solution.py
+++ b/solution.py
@@ -14,8 +14,11 @@
 WIDTH = STATIONS * NYW
 TA = 8
 MESH = pl.DeviceIdType.MESH
-CUTS = (0, 384, 896, 1280, 1792)
-CHUNKS = len(CUTS) - 1
+SENT = ((0, 1), (2, 3), (4, 5), (6,), (7,))
+CUTS = (0, 384, 896, 1280, 1536, 1792)
+DONE = (0, 256, 896, 1152, 1408, 1792)
+CHUNKS = len(SENT)
+AHEAD = 2
 KEPT = 5
 PAIR = 6
 
@@ -25,21 +28,14 @@
 
 
 def gram_kernel(
-    rows, total, x_ref, taps_ref, part_ref, out_ref,
-    sums, send, lines, gram, landed,
-    sum_send, sum_recv, line_send, line_recv, line_own, gram_send, gram_recv, gram_own,
+    rows, total, groups, x_ref, weight_ref, coef_ref, start_ref, end_ref, out_ref,
+    send, lines, scaled, taps, mean, base, gram, landed,
+    line_send, line_recv, line_own, gram_send, gram_recv, gram_own,
 ):
     place = lax.axis_index("gx")
     me = lax.axis_index("ta")
     wide = KEPT * rows
-
-    for span in range(SPAN):
-        def add(step, acc):
-            start = pl.multiple_of(step * 16, 16)
-            tile = x_ref[span, pl.ds(start, 16), :].astype(jnp.float32)
-            return acc + tile[:8] + tile[8:]
-        acc = lax.fori_loop(0, rows // 16, add, jnp.zeros((8, WIDTH), jnp.float32))
-        sums[me, pl.ds(span, 1), :] = jnp.sum(acc, axis=0, keepdims=True)
+    tall = 2 * rows
 
     barrier = pltpu.get_barrier_semaphore()
 
@@ -48,24 +44,6 @@
         pl.semaphore_signal(
             barrier, inc=1, device_id=(place, rotated(me, step, TA)), device_id_type=MESH
         )
-    pl.semaphore_wait(barrier, TA - 1)
-
-    def sum_copy(owner, target):
-        return pltpu.make_async_remote_copy(
-            src_ref=sums.at[owner], dst_ref=sums.at[owner],
-            send_sem=sum_send.at[target], recv_sem=sum_recv.at[owner],
-            device_id=(place, target), device_id_type=MESH,
-        )
-
-    @pl.loop(1, TA)
-    def _(step):
-        sum_copy(me, rotated(me, step, TA)).start()
-
-    @pl.loop(1, TA)
-    def _(step):
-        sum_copy(rotated(me, step, TA), me).wait_recv()
-
-    mean = jnp.sum(sums[...], axis=0) * (1.0 / total)
 
     def line_copy(chunk, owner, target):
         lanes = slice(CUTS[chunk], CUTS[chunk + 1])
@@ -84,29 +62,42 @@
             line_own.at[chunk],
         )
 
+    def start_lines(chunk):
+        @pl.loop(1, TA)
+        def _(step):
+            line_copy(chunk, me, rotated(me, step, TA)).start()
+
     for chunk in range(CHUNKS):
-        for span in (2 * chunk, 2 * chunk + 1):
-            level = mean[span : span + 1]
+        for span in SENT[chunk]:
 
             @pl.loop(0, rows // 16)
             def _(step):
                 start = pl.multiple_of(step * 16, 16)
-                centered = x_ref[span, pl.ds(start, 16), :].astype(jnp.float32) - level
-                filtered = taps_ref[BAND : BAND + 1, :] * centered
-                for offset in range(2 * BAND + 1):
-                    if offset != BAND:
-                        moved = pltpu.roll(centered, (BAND - offset) % WIDTH, 1)
-                        filtered = filtered + taps_ref[offset : offset + 1, :] * moved
-                scaled = filtered.astype(jnp.bfloat16)
+                tile = x_ref[span, pl.ds(start, 16), :]
                 for station in range(STATIONS):
-                    send[station, pl.ds(start, 16), NYW * span : NYW * (span + 1)] = scaled[
+                    send[station, pl.ds(start, 16), NYW * span : NYW * (span + 1)] = tile[
                         :, NYW * station : NYW * (station + 1)
                     ]
 
-        @pl.loop(1, TA)
-        def _(step):
-            line_copy(chunk, me, rotated(me, step, TA)).start()
+        if chunk == 0:
+            pl.semaphore_wait(barrier, TA - 1)
+
+        if chunk < AHEAD:
+            start_lines(chunk)
         own_copy(chunk).start()
+
+    weight = jnp.zeros((1, NYW), jnp.float32)
+    for station in range(STATIONS):
+        weight = jnp.where(
+            me == station, weight_ref[:, NYW * station : NYW * (station + 1)], weight
+        )
+    reach = (
+        lax.broadcasted_iota(jnp.int32, (2 * BAND + 1, NYW), 1)
+        + lax.broadcasted_iota(jnp.int32, (2 * BAND + 1, NYW), 0) - BAND
+    )
+    tap = jnp.where((reach >= 0) & (reach < NYW), coef_ref[...], 0.0) * jnp.sqrt(weight)
+    for span in range(SPAN):
+        taps[:, NYW * span : NYW * (span + 1)] = tap
 
     def gram_copy(owner, target):
         source = gram.at[
@@ -128,21 +119,61 @@
 
     pair = 2 * rows
     for chunk in range(CHUNKS):
-        lanes = slice(CUTS[chunk], CUTS[chunk + 1])
         own_copy(chunk).wait()
 
         @pl.loop(1, TA)
         def _(step):
             line_copy(chunk, rotated(me, step, TA), me).wait_recv()
+
+        if chunk + AHEAD < CHUNKS:
+
+            @pl.loop(1, TA)
+            def _(step):
+                line_copy(chunk, me, rotated(me, step, TA)).wait_send()
+            start_lines(chunk + AHEAD)
+
+        new = slice(CUTS[chunk], CUTS[chunk + 1])
+        fresh = CUTS[chunk + 1] - CUTS[chunk]
+
+        def add(step, acc):
+            start = pl.multiple_of(step * 16, 16)
+            tile = lines[pl.ds(start, 16), new].astype(jnp.float32)
+            return acc + tile
+        acc = lax.fori_loop(0, total // 16, add, jnp.zeros((16, fresh), jnp.float32))
+        mean[:, new] = jnp.sum(acc, axis=0, keepdims=True) * (1.0 / total)
+
+        first, last = DONE[chunk], DONE[chunk + 1]
+        low = first if first % (4 * NYW) == 0 else first - 128
+        high = last if last % (4 * NYW) == 0 else last + 128
+        lanes = slice(first, last)
+
+        middle = slice(first - low, last - low)
+        level = mean[:, low:high]
+        offset_level = jnp.zeros((1, last - first), jnp.float32)
+        for offset in range(2 * BAND + 1):
+            moved = level if offset == BAND else pltpu.roll(level, (BAND - offset) % (high - low), 1)
+            offset_level = offset_level + taps[offset : offset + 1, lanes] * moved[:, middle]
+        base[:, lanes] = offset_level
+
+        @pl.loop(0, total // tall)
+        def _(step):
+            at = pl.ds(pl.multiple_of(step * tall, tall), tall)
+            raw = lines[at, low:high]
+            filtered = taps[BAND : BAND + 1, lanes] * raw[:, middle].astype(jnp.float32)
+            for offset in range(2 * BAND + 1):
+                if offset != BAND:
+                    moved = pltpu.roll(raw, (BAND - offset) % (high - low), 1)[:, middle]
+                    filtered = filtered + taps[offset : offset + 1, lanes] * moved.astype(jnp.float32)
+            scaled[at, lanes] = (filtered - base[:, lanes]).astype(jnp.bfloat16)
 
         @pl.loop(1, TA // 2 + 1)
         def _(step):
             row = lax.rem(me // 2 + step, TA // 2)
             where = pl.ds(pl.multiple_of(row * pair, pair), pair)
-            left = lines[where, lanes]
+            left = scaled[where, lanes]
             for block in range(PAIR // 2):
                 column = lax.rem(row + block, TA // 2)
-                right = lines[pl.ds(pl.multiple_of(column * pair, pair), pair), lanes]
+                right = scaled[pl.ds(pl.multiple_of(column * pair, pair), pair), lanes]
                 product = lax.dot_general(
                     left, right, (((1,), (1,)), ((), ())), preferred_element_type=jnp.float32
                 )
@@ -162,20 +193,32 @@
     gram_local().start()
     gram_local().wait()
 
+    next_start = jnp.where(
+        place + 1 < groups, start_ref[jnp.minimum(place + 1, groups - 1)], groups * STATIONS
+    )
+    last_end = jnp.where(place > 0, end_ref[jnp.maximum(place - 1, 0)], 0)
+
+    def shares(owner):
+        station = place * STATIONS + owner
+        upper = jnp.where(station >= next_start, 1.0, 0.0)
+        lower = jnp.where(station < last_end, 1.0, 0.0)
+        return upper, lower
+
+    upper, lower = shares(me)
+
     @pl.loop(0, rows // 8)
     def _(step):
         at = pl.ds(pl.multiple_of(step * 8, 8), 8)
         tile = landed[me, at, :]
         out_ref[0, at, :] = tile
-        out_ref[1, at, :] = tile * part_ref[0, me]
-        out_ref[2, at, :] = tile * part_ref[1, me]
+        out_ref[1, at, :] = tile * upper
+        out_ref[2, at, :] = tile * lower
 
     @pl.loop(1, TA)
     def _(count):
         owner = rotated(me, TA - count, TA)
         gram_copy(owner, me).wait_recv()
-        upper = part_ref[0, owner]
-        lower = part_ref[1, owner]
+        upper, lower = shares(owner)
 
         @pl.loop(0, rows // 8)
         def _(step):
@@ -188,14 +231,14 @@
     @pl.loop(1, TA)
     def _(step):
         target = rotated(me, step, TA)
-        sum_copy(me, target).wait_send()
         gram_copy(me, target).wait_send()
-        for chunk in range(CHUNKS):
+        for chunk in range(CHUNKS - AHEAD, CHUNKS):
             line_copy(chunk, me, target).wait_send()
 
 
 def owner_kernel(
-    groups, rows, sums_ref, source_ref, count_ref, out_ref,
+    groups, rows, sums_ref, start_ref, end_ref, owner_ref, out_ref,
+    source,
     beside, pieces, spread, ordered, owned, block, turned,
     side_send, side_recv, out_send, out_recv, back_send, back_recv, turn_send, turn_recv, own_sem,
 ):
@@ -228,13 +271,22 @@
 
     for side in range(2):
         side_copy(side).start()
+
+    @pl.loop(0, groups)
+    def _(slot):
+        window = jnp.int32(0)
+        for step in range(groups):
+            window = jnp.where(owner_ref[step] == slot, step, window)
+        source[slot] = window
+    count = ((end_ref[place] - start_ref[place]) * (SPAN * NYW)).astype(jnp.float32)
+
     for side in range(2):
         side_copy(side).wait()
 
     @pl.loop(0, rows // 8)
     def _(step):
         at = pl.ds(pl.multiple_of(step * 8, 8), 8)
-        tile = (sums_ref[0, at, :] + beside[0, at, :] + beside[1, at, :]) / count_ref[0]
+        tile = (sums_ref[0, at, :] + beside[0, at, :] + beside[1, at, :]) / count
         for part in range(8 // piece):
             pieces[step * (8 // piece) + part] = tile[part * piece : (part + 1) * piece]
 
@@ -258,7 +310,7 @@
 
     @pl.loop(0, groups)
     def _(slot):
-        ordered[slot] = spread[source_ref[slot]]
+        ordered[slot] = spread[source[slot]]
 
     def back_copy(owner, target):
         return pltpu.make_async_remote_copy(
@@ -317,40 +369,25 @@
     groups = lax.axis_size("gx")
     piece = rows // groups
     total = rows * TA
-    place = lax.axis_index("gx")
-
     lines = jnp.transpose(field, (1, 0, 2))
-    point = jnp.arange(NYW, dtype=jnp.int32)[None, :]
-    reach = point + jnp.arange(-BAND, BAND + 1, dtype=jnp.int32)[:, None]
-    taps = jnp.where((reach >= 0) & (reach < NYW), coef, 0.0)
-    taps = jnp.tile(taps, (1, STATIONS)) * jnp.sqrt(weight)[None, :]
-
-    station = place * STATIONS + jnp.arange(STATIONS, dtype=jnp.int32)
-    next_start = jnp.where(
-        place + 1 < groups, window_start[jnp.minimum(place + 1, groups - 1)], groups * STATIONS
-    )
-    last_end = jnp.where(place > 0, window_end[jnp.maximum(place - 1, 0)], 0)
-    part = jnp.stack([station >= next_start, station < last_end]).astype(jnp.float32)
-    count = ((window_end[place] - window_start[place]) * SPAN * NYW).astype(jnp.float32)
-    order = jnp.arange(groups, dtype=jnp.int32)
-    source = jnp.sum(jnp.where(owner_map[None, :] == order[:, None], order[None, :], 0), axis=1)
-
     vmem = pl.BlockSpec(memory_space=pltpu.VMEM)
     smem = pl.BlockSpec(memory_space=pltpu.SMEM)
     dma = pltpu.SemaphoreType.DMA
     wide = KEPT * rows
     sums = pl.pallas_call(
-        functools.partial(gram_kernel, rows, total),
+        functools.partial(gram_kernel, rows, total, groups),
         out_shape=jax.ShapeDtypeStruct((3, rows, wide), jnp.float32),
-        in_specs=[vmem, vmem, smem],
+        in_specs=[vmem, vmem, vmem, smem, smem],
         out_specs=vmem,
         scratch_shapes=[
-            pltpu.VMEM((TA, SPAN, WIDTH), jnp.float32),
             pltpu.VMEM((TA, rows, WIDTH), jnp.bfloat16),
             pltpu.VMEM((total, WIDTH), jnp.bfloat16),
+            pltpu.VMEM((total, WIDTH), jnp.bfloat16),
+            pltpu.VMEM((2 * BAND + 1, WIDTH), jnp.float32),
+            pltpu.VMEM((1, WIDTH), jnp.float32),
+            pltpu.VMEM((1, WIDTH), jnp.float32),
             pltpu.VMEM((total, PAIR * rows), jnp.float32),
             pltpu.VMEM((TA, rows, wide), jnp.float32),
-            dma((TA,)), dma((TA,)),
             dma((CHUNKS, TA)), dma((CHUNKS, TA)), dma((CHUNKS,)),
             dma((TA,)), dma((TA,)), dma,
         ],
@@ -358,15 +395,16 @@
             collective_id=0, has_side_effects=True, vmem_limit_bytes=48 * 1024 * 1024
         ),
         name="station_gram",
-    )(lines, taps, part)
+    )(lines, weight[None], coef, window_start, window_end)
 
     turns = TA - KEPT
     owned = pl.pallas_call(
         functools.partial(owner_kernel, groups, rows),
         out_shape=jax.ShapeDtypeStruct((rows, total), jnp.float32),
-        in_specs=[vmem, smem, smem],
+        in_specs=[vmem, smem, smem, smem],
         out_specs=vmem,
         scratch_shapes=[
+            pltpu.SMEM((groups,), jnp.int32),
             pltpu.VMEM((2, rows, wide), jnp.float32),
             pltpu.VMEM((groups, piece, wide), jnp.float32),
             pltpu.VMEM((groups, piece, wide), jnp.float32),
@@ -381,7 +419,7 @@
             collective_id=1, has_side_effects=True, vmem_limit_bytes=32 * 1024 * 1024
         ),
         name="owner_rows",
-    )(sums, source, count[None])
+    )(sums, window_start, window_end, owner_map)
     return owned[None]
 
 

time: 149 us -> 134 us (0.90); the launches traced: 146 us -> 134 us
  Pallas kernels: 137 us -> 129 us
  between operations: 2.6 us -> 0.08 us
  other arithmetic: 1.58 us -> 0 us
    pallas_call x1, Pallas kernels: 86.4 us -> 77.9 us  [on_device(): pl.pallas_call(functools.partial(gram_kernel, rows, total, groups), out_s...]
    unnamed x2 -> x10, local copies, waits for them, and re-layouts: 3.51 us -> 3.55 us
where the time goes in v3:
time: 134 us
  Pallas kernels  129 us (96%)
  local copies, waits for them, and re-layouts  4.25 us (3%)
    pallas_call x1, Pallas kernels, on_device(): pl.pallas_call(functools.partial(gram_kernel, rows, total, groups), out_s...  77.9 us
    pallas_call x1, Pallas kernels, on_device(): pl.pallas_call(functools.partial(owner_kernel, groups, rows), out_shape=j...  51.5 us
    unnamed x10, local copies, waits for them, and re-layouts  3.55 us

profile of v3, /device:TPU:2, one launch (start us, length us, event | category | flops | bytes accessed | tf_op | source)
XLA Modules:
  0.0 133.7 jit_solution(15845643794316174620)
XLA Ops:
  0.0 0.7 broadcast_in_dim.6.weight_ref
  0.7 0.0 copy-start
  0.7 0.0 copy-start.1
  0.7 0.0 copy-start.2
  0.7 2.7 %copy.9 = bf16[128,8,1792]{2,0,1:T(8,128)(2,1)S(1)} copy(bf16[128,8,1792]{2,1,0:T(8,128)(2,1)} %param.6) | data formatting | bytes 7340032 | tf_op args[0]
  3.5 0.0 copy-start.3
  3.5 0.0 copy-done
  3.5 0.0 copy-done.1
  3.5 0.0 copy-done.2
  3.5 77.9 %station_gram.1.sums_ref = f32[3,128,640]{2,1,0:T(8,128)S(1)} custom-call(bf16[8,128,1792]{2,1,0:T(8,128)(2,1)S(1)} %bitcast.4, f32[1,1792]{1,0:T(1,128)S(1)} %broadcast_in_dim.6.weight_ref, f32[5,224]{1,0:T(8,128)S(1)} %copy-done, s32[32]{0:T(128)S(1)} %copy-done.1, s32[32]{0:T(128)S(1)} %copy-done.2), custom_call_target="tpu_custom_call" | custom-call | tf_op jit(solution)/shard_map/station_gram/pallas_call | solution.py:377
  81.4 0.0 copy-done.3
  81.4 51.5 %owner_rows.1 = f32[128,1024]{1,0:T(8,128)S(1)} custom-call(f32[3,128,640]{2,1,0:T(8,128)S(1)} %station_gram.1.sums_ref, s32[32]{0:T(128)S(1)} %copy-done.1, s32[32]{0:T(128)S(1)} %copy-done.2, s32[32]{0:T(128)S(1)} %copy-done.3), custom_call_target="tpu_custom_call" | custom-call | tf_op jit(solution)/shard_map/owner_rows/pallas_call | solution.py:401
  132.9 0.8 copy.11
Async XLA Ops:
  0.7 2.8 %copy-start = (f32[5,224]{1,0:T(8,128)S(1)}, f32[5,224]{1,0:T(8,128)}, u32[]{:S(2)}) copy-start(f32[5,224]{1,0:T(8,128)} %coef_ref.1) | copy-start | bytes 13444
  0.7 2.8 %copy-start.1 = (s32[32]{0:T(128)S(1)}, s32[32]{0:T(128)}, u32[]{:S(2)}) copy-start(s32[32]{0:T(128)} %start_ref.3) | copy-start | bytes 388
  0.7 2.8 %copy-start.2 = (s32[32]{0:T(128)S(1)}, s32[32]{0:T(128)}, u32[]{:S(2)}) copy-start(s32[32]{0:T(128)} %end_ref.3) | copy-start | bytes 388
  3.5 77.9 %copy-start.3 = (s32[32]{0:T(128)S(1)}, s32[32]{0:T(128)}, u32[]{:S(2)}) copy-start(s32[32]{0:T(128)} %owner_ref.1) | copy-start | bytes 388

commit v4 on v3

v4 whole, which is shorter than its diff:
```python
import functools

import jax
import jax.numpy as jnp
from jax import lax
from jax.experimental import pallas as pl
from jax.experimental.pallas import tpu as pltpu
from jax.sharding import PartitionSpec as P

SPAN = 8
NYW = 224
BAND = 2
STATIONS = 8
WIDTH = STATIONS * NYW
TA = 8
MESH = pl.DeviceIdType.MESH
SENT = ((0, 1), (2, 3), (4, 5), (6,), (7,))
CUTS = (0, 384, 896, 1280, 1536, 1792)
DONE = (0, 256, 896, 1152, 1408, 1792)
CHUNKS = len(SENT)
AHEAD = 2
KEPT = 5
PAIR = 6
PARTS = ((0, 3), (3, 5))


def rotated(me, step, count):
    return lax.rem(me + step, count)


def window_kernel(
    rows, total, groups, x_ref, weight_ref, coef_ref, start_ref, end_ref, owner_ref, out_ref,
    source, send, lines, scaled, taps, mean, base, gram, block, turned,
    line_send, line_recv, line_own, gram_send, gram_recv, gram_own,
    side_send, side_recv, out_send, out_recv, out_own, back_send, back_recv, back_own,
    turn_send, turn_recv, *parts,
):
    place = lax.axis_index("gx")
    me = lax.axis_index("ta")
    tall = 2 * rows
    piece = rows // groups
    turns = TA - KEPT
    landed, summed, beside, pieces, spread, ordered, owned = (
        parts[2 * kind : 2 * kind + 2] for kind in range(7)
    )

    barrier = pltpu.get_barrier_semaphore()

    @pl.loop(1, TA)
    def _(step):
        pl.semaphore_signal(
            barrier, inc=1, device_id=(place, rotated(me, step, TA)), device_id_type=MESH
        )

    @pl.loop(1, groups)
    def _(step):
        pl.semaphore_signal(
            barrier, inc=1, device_id=(rotated(place, step, groups), me), device_id_type=MESH
        )

    def line_copy(chunk, owner, target):
        lanes = slice(CUTS[chunk], CUTS[chunk + 1])
        return pltpu.make_async_remote_copy(
            src_ref=send.at[target, :, lanes],
            dst_ref=lines.at[pl.ds(pl.multiple_of(owner * rows, rows), rows), lanes],
            send_sem=line_send.at[chunk, target], recv_sem=line_recv.at[chunk, owner],
            device_id=(place, target), device_id_type=MESH,
        )

    def own_copy(chunk):
        lanes = slice(CUTS[chunk], CUTS[chunk + 1])
        return pltpu.make_async_copy(
            send.at[me, :, lanes],
            lines.at[pl.ds(pl.multiple_of(me * rows, rows), rows), lanes],
            line_own.at[chunk],
        )

    def start_lines(chunk):
        @pl.loop(1, TA)
        def _(step):
            line_copy(chunk, me, rotated(me, step, TA)).start()

    for chunk in range(CHUNKS):
        for span in SENT[chunk]:

            @pl.loop(0, rows // 16)
            def _(step):
                start = pl.multiple_of(step * 16, 16)
                tile = x_ref[span, pl.ds(start, 16), :]
                for station in range(STATIONS):
                    send[station, pl.ds(start, 16), NYW * span : NYW * (span + 1)] = tile[
                        :, NYW * station : NYW * (station + 1)
                    ]

        if chunk == 0:
            pl.semaphore_wait(barrier, TA - 1 + groups - 1)

        if chunk < AHEAD:
            start_lines(chunk)
        own_copy(chunk).start()

    weight = jnp.zeros((1, NYW), jnp.float32)
    for station in range(STATIONS):
        weight = jnp.where(
            me == station, weight_ref[:, NYW * station : NYW * (station + 1)], weight
        )
    reach = (
        lax.broadcasted_iota(jnp.int32, (2 * BAND + 1, NYW), 1)
        + lax.broadcasted_iota(jnp.int32, (2 * BAND + 1, NYW), 0) - BAND
    )
    tap = jnp.where((reach >= 0) & (reach < NYW), coef_ref[...], 0.0) * jnp.sqrt(weight)
    for span in range(SPAN):
        taps[:, NYW * span : NYW * (span + 1)] = tap

    def gram_rows(part, target):
        low, high = PARTS[part]
        begin = (lax.rem(target, 2) + low) * rows
        return gram.at[
            pl.ds(pl.multiple_of(target * rows, rows), rows),
            pl.ds(pl.multiple_of(begin, rows), (high - low) * rows),
        ]

    def gram_copy(part, owner, target):
        return pltpu.make_async_remote_copy(
            src_ref=gram_rows(part, target), dst_ref=landed[part].at[owner],
            send_sem=gram_send.at[part, target], recv_sem=gram_recv.at[part, owner],
            device_id=(place, target), device_id_type=MESH,
        )

    def gram_local(part):
        return pltpu.make_async_copy(gram_rows(part, me), landed[part].at[me], gram_own.at[part])

    def to_others(row, act):
        for side in range(2):
            target = 2 * row + side

            @pl.when(target != me)
            def _():
                act(target)

    pair = 2 * rows
    for chunk in range(CHUNKS):
        own_copy(chunk).wait()

        @pl.loop(1, TA)
        def _(step):
            line_copy(chunk, rotated(me, step, TA), me).wait_recv()

        if chunk + AHEAD < CHUNKS:

            @pl.loop(1, TA)
            def _(step):
                line_copy(chunk, me, rotated(me, step, TA)).wait_send()
            start_lines(chunk + AHEAD)

        new = slice(CUTS[chunk], CUTS[chunk + 1])
        fresh = CUTS[chunk + 1] - CUTS[chunk]

        def add(step, acc):
            start = pl.multiple_of(step * 16, 16)
            tile = lines[pl.ds(start, 16), new].astype(jnp.float32)
            return acc + tile
        acc = lax.fori_loop(0, total // 16, add, jnp.zeros((16, fresh), jnp.float32))
        mean[:, new] = jnp.sum(acc, axis=0, keepdims=True) * (1.0 / total)

        first, last = DONE[chunk], DONE[chunk + 1]
        low = first if first % (4 * NYW) == 0 else first - 128
        high = last if last % (4 * NYW) == 0 else last + 128
        lanes = slice(first, last)

        middle = slice(first - low, last - low)
        level = mean[:, low:high]
        offset_level = jnp.zeros((1, last - first), jnp.float32)
        for offset in range(2 * BAND + 1):
            moved = level if offset == BAND else pltpu.roll(level, (BAND - offset) % (high - low), 1)
            offset_level = offset_level + taps[offset : offset + 1, lanes] * moved[:, middle]
        base[:, lanes] = offset_level

        @pl.loop(0, total // tall)
        def _(step):
            at = pl.ds(pl.multiple_of(step * tall, tall), tall)
            raw = lines[at, low:high]
            filtered = taps[BAND : BAND + 1, lanes] * raw[:, middle].astype(jnp.float32)
            for offset in range(2 * BAND + 1):
                if offset != BAND:
                    moved = pltpu.roll(raw, (BAND - offset) % (high - low), 1)[:, middle]
                    filtered = filtered + taps[offset : offset + 1, lanes] * moved.astype(jnp.float32)
            scaled[at, lanes] = (filtered - base[:, lanes]).astype(jnp.bfloat16)

        def multiply(row, blocks):
            where = pl.ds(pl.multiple_of(row * pair, pair), pair)
            left = scaled[where, lanes]
            for index in blocks:
                column = lax.rem(row + index, TA // 2)
                right = scaled[pl.ds(pl.multiple_of(column * pair, pair), pair), lanes]
                product = lax.dot_general(
                    left, right, (((1,), (1,)), ((), ())), preferred_element_type=jnp.float32
                )
                at = slice(index * pair, (index + 1) * pair)
                if chunk == 0:
                    gram[where, at] = product
                else:
                    gram[where, at] = gram[where, at] + product

        if chunk < CHUNKS - 1:

            @pl.loop(0, TA // 2)
            def _(row):
                multiply(row, range(PAIR // 2))
        else:

            @pl.loop(1, TA // 2 + 1)
            def _(step):
                row = lax.rem(me // 2 + step, TA // 2)
                multiply(row, (0, 1))
                to_others(row, lambda target: gram_copy(0, me, target).start())
            gram_local(0).start()

            @pl.loop(0, TA // 2)
            def _(row):
                multiply(row, (2,))

    gram_local(1).start()

    @pl.loop(0, groups)
    def _(slot):
        window = jnp.int32(0)
        for step in range(groups):
            window = jnp.where(owner_ref[step] == slot, step, window)
        source[slot] = window
    count = ((end_ref[place] - start_ref[place]) * (SPAN * NYW)).astype(jnp.float32)

    @pl.loop(1, TA // 2 + 1)
    def _(step):
        row = lax.rem(me // 2 + step, TA // 2)

        def follow(target):
            gram_copy(0, me, target).wait_send()
            gram_copy(1, me, target).start()
        to_others(row, follow)

    next_start = jnp.where(
        place + 1 < groups, start_ref[jnp.minimum(place + 1, groups - 1)], groups * STATIONS
    )
    last_end = jnp.where(place > 0, end_ref[jnp.maximum(place - 1, 0)], 0)

    def shares(owner):
        station = place * STATIONS + owner
        upper = jnp.where(station >= next_start, 1.0, 0.0)
        lower = jnp.where(station < last_end, 1.0, 0.0)
        return upper, lower

    def reduce_part(part):
        land, total_of = landed[part], summed[part]
        gram_local(part).wait()
        upper, lower = shares(me)

        @pl.loop(0, rows // 8)
        def _(step):
            at = pl.ds(pl.multiple_of(step * 8, 8), 8)
            tile = land[me, at, :]
            total_of[0, at, :] = tile
            total_of[1, at, :] = tile * upper
            total_of[2, at, :] = tile * lower

        @pl.loop(1, TA)
        def _(count):
            owner = rotated(me, TA - count, TA)
            gram_copy(part, owner, me).wait_recv()
            upper, lower = shares(owner)

            @pl.loop(0, rows // 8)
            def _(step):
                at = pl.ds(pl.multiple_of(step * 8, 8), 8)
                tile = land[owner, at, :]
                total_of[0, at, :] = total_of[0, at, :] + tile
                total_of[1, at, :] = total_of[1, at, :] + tile * upper
                total_of[2, at, :] = total_of[2, at, :] + tile * lower

    after = rotated(place, 1, groups)
    before = rotated(place, groups - 1, groups)

    def side_copy(part, side):
        return pltpu.make_async_remote_copy(
            src_ref=summed[part].at[1 + side], dst_ref=beside[part].at[side],
            send_sem=side_send.at[part, side], recv_sem=side_recv.at[part, side],
            device_id=((after, before)[side], me), device_id_type=MESH,
        )

    def out_copy(part, owner, target):
        return pltpu.make_async_remote_copy(
            src_ref=pieces[part].at[target], dst_ref=spread[part].at[owner],
            send_sem=out_send.at[part, target], recv_sem=out_recv.at[part, owner],
            device_id=(target, me), device_id_type=MESH,
        )

    def out_local(part):
        return pltpu.make_async_copy(
            pieces[part].at[place], spread[part].at[place], out_own.at[part]
        )

    def back_copy(part, owner, target):
        return pltpu.make_async_remote_copy(
            src_ref=ordered[part].at[target], dst_ref=owned[part].at[owner],
            send_sem=back_send.at[part, target], recv_sem=back_recv.at[part, owner],
            device_id=(target, me), device_id_type=MESH,
        )

    def back_local(part):
        return pltpu.make_async_copy(
            ordered[part].at[place], owned[part].at[place], back_own.at[part]
        )

    for part in range(2):
        reduce_part(part)
        for side in range(2):
            side_copy(part, side).start()
        for side in range(2):
            side_copy(part, side).wait()

        @pl.loop(0, rows // 8)
        def _(step):
            at = pl.ds(pl.multiple_of(step * 8, 8), 8)
            tile = (summed[part][0, at, :] + beside[part][0, at, :] + beside[part][1, at, :]) / count
            for half in range(8 // piece):
                pieces[part][step * (8 // piece) + half] = tile[half * piece : (half + 1) * piece]

        @pl.loop(1, groups)
        def _(step):
            out_copy(part, place, rotated(place, step, groups)).start()
        out_local(part).start()

    for part in range(2):
        out_local(part).wait()

        @pl.loop(1, groups)
        def _(step):
            out_copy(part, rotated(place, groups - step, groups), place).wait_recv()

        @pl.loop(0, groups)
        def _(slot):
            ordered[part][slot] = spread[part][source[slot]]

        @pl.loop(1, groups)
        def _(step):
            back_copy(part, place, rotated(place, step, groups)).start()
        back_local(part).start()

    def turn_copy(turn):
        return pltpu.make_async_remote_copy(
            src_ref=block.at[turn], dst_ref=turned.at[turn - 1],
            send_sem=turn_send.at[turn - 1], recv_sem=turn_recv.at[turn - 1],
            device_id=(place, rotated(me, turn, TA)), device_id_type=MESH,
        )

    for part in range(2):
        low, high = PARTS[part]
        back_local(part).wait()

        @pl.loop(1, groups)
        def _(step):
            back_copy(part, rotated(place, groups - step, groups), place).wait_recv()

        @pl.loop(0, rows // 8)
        def _(step):
            for half in range(8 // piece):
                tile = owned[part][step * (8 // piece) + half]
                for column in range(low, high):
                    block[column, pl.ds(step * 8 + half * piece, piece), :] = tile[
                        :, (column - low) * rows : (column - low + 1) * rows
                    ]

        for column in range(low, high):
            if 1 <= column <= turns:
                turn_copy(column).start()
        for column in range(low, high):
            target = rotated(me, column, TA)
            out_ref[:, pl.ds(pl.multiple_of(target * rows, rows), rows)] = block[column]

    for turn in range(1, turns + 1):
        turn_copy(turn).wait()
        target = rotated(me, TA - turn, TA)
        out_ref[:, pl.ds(pl.multiple_of(target * rows, rows), rows)] = turned[turn - 1].T

    @pl.loop(1, TA)
    def _(step):
        target = rotated(me, step, TA)
        gram_copy(1, me, target).wait_send()
        for chunk in range(CHUNKS - AHEAD, CHUNKS):
            line_copy(chunk, me, target).wait_send()

    @pl.loop(1, groups)
    def _(step):
        target = rotated(place, step, groups)
        for part in range(2):
            out_copy(part, place, target).wait_send()
            back_copy(part, place, target).wait_send()


def on_device(field, weight, coef, window_start, window_end, owner_map):
    rows = field.shape[0]
    groups = lax.axis_size("gx")
    piece = rows // groups
    total = rows * TA
    lines = jnp.transpose(field, (1, 0, 2))
    vmem = pl.BlockSpec(memory_space=pltpu.VMEM)
    smem = pl.BlockSpec(memory_space=pltpu.SMEM)
    dma = pltpu.SemaphoreType.DMA
    turns = TA - KEPT
    widths = [(high - low) * rows for low, high in PARTS]

    def part_scratch(*shape):
        return [pltpu.VMEM((*shape, width), jnp.float32) for width in widths]

    owned = pl.pallas_call(
        functools.partial(window_kernel, rows, total, groups),
        out_shape=jax.ShapeDtypeStruct((rows, total), jnp.float32),
        in_specs=[vmem, vmem, vmem, smem, smem, smem],
        out_specs=vmem,
        scratch_shapes=[
            pltpu.SMEM((groups,), jnp.int32),
            pltpu.VMEM((TA, rows, WIDTH), jnp.bfloat16),
            pltpu.VMEM((total, WIDTH), jnp.bfloat16),
            pltpu.VMEM((total, WIDTH), jnp.bfloat16),
            pltpu.VMEM((2 * BAND + 1, WIDTH), jnp.float32),
            pltpu.VMEM((1, WIDTH), jnp.float32),
            pltpu.VMEM((1, WIDTH), jnp.float32),
            pltpu.VMEM((total, PAIR * rows), jnp.float32),
            pltpu.VMEM((KEPT, rows, rows), jnp.float32),
            pltpu.VMEM((turns, rows, rows), jnp.float32),
            dma((CHUNKS, TA)), dma((CHUNKS, TA)), dma((CHUNKS,)),
            dma((2, TA)), dma((2, TA)), dma((2,)),
            dma((2, 2)), dma((2, 2)),
            dma((2, groups)), dma((2, groups)), dma((2,)),
            dma((2, groups)), dma((2, groups)), dma((2,)),
            dma((turns,)), dma((turns,)),
            *part_scratch(TA, rows),
            *part_scratch(3, rows),
            *part_scratch(2, rows),
            *part_scratch(groups, piece),
            *part_scratch(groups, piece),
            *part_scratch(groups, piece),
            *part_scratch(groups, piece),
        ],
        compiler_params=pltpu.CompilerParams(
            collective_id=0, has_side_effects=True, vmem_limit_bytes=48 * 1024 * 1024
        ),
        name="window_rows",
    )(lines, weight[None], coef, window_start, window_end, owner_map)
    return owned[None]


def solution(mesh):
    placed = (P("ta", None, "gx"), P("gx"), P(), P(), P(), P())
    return jax.shard_map(
        on_device, mesh=mesh, in_specs=placed, out_specs=P("gx", "ta", None), check_vma=False
    )
```

time: 134 us -> 120 us (0.90)
  Pallas kernels: 129 us -> 114 us
    pallas_call x2 -> x1, Pallas kernels: 129 us -> 114 us  [on_device(): pl.pallas_call(functools.partial(window_kernel, rows, total, groups), out...]
where the time goes in v4:
time: 120 us; the launch traced here: 119 us
  Pallas kernels  114 us (95%)
  local copies, waits for them, and re-layouts  4.26 us (4%)
    pallas_call x1, Pallas kernels, on_device(): pl.pallas_call(functools.partial(window_kernel, rows, total, groups), out...  114 us
    unnamed x10, local copies, waits for them, and re-layouts  3.56 us

profile of v4, /device:TPU:2, one launch (start us, length us, event | category | flops | bytes accessed | tf_op | source)
XLA Modules:
  0.0 118.8 jit_solution(17867731398236871714)
XLA Ops:
  0.0 0.7 broadcast_in_dim.6.weight_ref
  0.7 0.0 copy-start
  0.7 0.0 copy-start.1
  0.7 0.0 copy-start.2
  0.7 0.0 copy-start.3
  0.7 2.7 %copy.9 = bf16[128,8,1792]{2,0,1:T(8,128)(2,1)S(1)} copy(bf16[128,8,1792]{2,1,0:T(8,128)(2,1)} %param.6) | data formatting | bytes 7340032 | tf_op args[0]
  3.5 0.0 copy-done
  3.5 0.0 copy-done.1
  3.5 0.0 copy-done.2
  3.5 0.0 copy-done.3
  3.5 114.5 %window_rows.1 = f32[128,1024]{1,0:T(8,128)S(1)} custom-call(bf16[8,128,1792]{2,1,0:T(8,128)(2,1)S(1)} %bitcast.4, f32[1,1792]{1,0:T(1,128)S(1)} %broadcast_in_dim.6.weight_ref, f32[5,224]{1,0:T(8,128)S(1)} %copy-done, s32[32]{0:T(128)S(1)} %copy-done.1, s32[32]{0:T(128)S(1)} %copy-done.2, s32[32]{0:T(128)S(1)} %copy-done.3), custom_call_target="tpu_custom_call" | custom-call | tf_op jit(solution)/shard_map/window_rows/pallas_call | solution.py:415
  118.0 0.8 copy.11
Async XLA Ops:
  0.7 2.8 %copy-start = (f32[5,224]{1,0:T(8,128)S(1)}, f32[5,224]{1,0:T(8,128)}, u32[]{:S(2)}) copy-start(f32[5,224]{1,0:T(8,128)} %coef_ref.1) | copy-start | bytes 13444
  0.7 2.8 %copy-start.1 = (s32[32]{0:T(128)S(1)}, s32[32]{0:T(128)}, u32[]{:S(2)}) copy-start(s32[32]{0:T(128)} %start_ref.1) | copy-start | bytes 388
  0.7 2.8 %copy-start.2 = (s32[32]{0:T(128)S(1)}, s32[32]{0:T(128)}, u32[]{:S(2)}) copy-start(s32[32]{0:T(128)} %end_ref.1) | copy-start | bytes 388
  0.7 2.8 %copy-start.3 = (s32[32]{0:T(128)S(1)}, s32[32]{0:T(128)}, u32[]{:S(2)}) copy-start(s32[32]{0:T(128)} %owner_ref.1) | copy-start | bytes 388

commit v5 on v4

--- a/solution.py
+++ b/solution.py
@@ -21,7 +21,10 @@
 AHEAD = 2
 KEPT = 5
 PAIR = 6
-PARTS = ((0, 3), (3, 5))
+PARTS = ((1, 4), (4, 5), (0, 1))
+COUNT = len(PARTS)
+GROUPED = ((0,), (1, 2))
+TRIPS = len(GROUPED)
 
 
 def rotated(me, step, count):
@@ -38,10 +41,13 @@
     place = lax.axis_index("gx")
     me = lax.axis_index("ta")
     tall = 2 * rows
+    tile_rows = max(rows // 2, 16)
     piece = rows // groups
     turns = TA - KEPT
-    landed, summed, beside, pieces, spread, ordered, owned = (
-        parts[2 * kind : 2 * kind + 2] for kind in range(7)
+    landed, summed, beside = (parts[COUNT * kind : COUNT * (kind + 1)] for kind in range(3))
+    parts = parts[COUNT * 3 :]
+    pieces, spread, ordered, owned = (
+        parts[TRIPS * kind : TRIPS * (kind + 1)] for kind in range(4)
     )
 
     barrier = pltpu.get_barrier_semaphore()
@@ -83,12 +89,12 @@
     for chunk in range(CHUNKS):
         for span in SENT[chunk]:
 
-            @pl.loop(0, rows // 16)
+            @pl.loop(0, rows // tile_rows)
             def _(step):
-                start = pl.multiple_of(step * 16, 16)
-                tile = x_ref[span, pl.ds(start, 16), :]
+                at = pl.ds(pl.multiple_of(step * tile_rows, tile_rows), tile_rows)
+                tile = x_ref[span, at, :]
                 for station in range(STATIONS):
-                    send[station, pl.ds(start, 16), NYW * span : NYW * (span + 1)] = tile[
+                    send[station, at, NYW * span : NYW * (span + 1)] = tile[
                         :, NYW * station : NYW * (station + 1)
                     ]
 
@@ -99,10 +105,12 @@
             start_lines(chunk)
         own_copy(chunk).start()
 
+    for tile in range(WIDTH // 128):
+        base[:, 128 * tile : 128 * (tile + 1)] = weight_ref[tile : tile + 1, :]
     weight = jnp.zeros((1, NYW), jnp.float32)
     for station in range(STATIONS):
         weight = jnp.where(
-            me == station, weight_ref[:, NYW * station : NYW * (station + 1)], weight
+            me == station, base[:, NYW * station : NYW * (station + 1)], weight
         )
     reach = (
         lax.broadcasted_iota(jnp.int32, (2 * BAND + 1, NYW), 1)
@@ -212,15 +220,11 @@
             @pl.loop(1, TA // 2 + 1)
             def _(step):
                 row = lax.rem(me // 2 + step, TA // 2)
-                multiply(row, (0, 1))
+                multiply(row, range(PAIR // 2))
                 to_others(row, lambda target: gram_copy(0, me, target).start())
-            gram_local(0).start()
-
-            @pl.loop(0, TA // 2)
-            def _(row):
-                multiply(row, (2,))
-
-    gram_local(1).start()
+
+    for part in range(COUNT):
+        gram_local(part).start()
 
     @pl.loop(0, groups)
     def _(slot):
@@ -230,14 +234,15 @@
         source[slot] = window
     count = ((end_ref[place] - start_ref[place]) * (SPAN * NYW)).astype(jnp.float32)
 
-    @pl.loop(1, TA // 2 + 1)
-    def _(step):
-        row = lax.rem(me // 2 + step, TA // 2)
-
-        def follow(target):
-            gram_copy(0, me, target).wait_send()
-            gram_copy(1, me, target).start()
-        to_others(row, follow)
+    def follow(part):
+        @pl.loop(1, TA // 2 + 1)
+        def _(step):
+            row = lax.rem(me // 2 + step, TA // 2)
+
+            def act(target):
+                gram_copy(part - 1, me, target).wait_send()
+                gram_copy(part, me, target).start()
+            to_others(row, act)
 
     next_start = jnp.where(
         place + 1 < groups, start_ref[jnp.minimum(place + 1, groups - 1)], groups * STATIONS
@@ -311,26 +316,38 @@
             ordered[part].at[place], owned[part].at[place], back_own.at[part]
         )
 
-    for part in range(2):
+    def send_sides(part):
         reduce_part(part)
         for side in range(2):
             side_copy(part, side).start()
-        for side in range(2):
-            side_copy(part, side).wait()
+
+    def send_pieces(trip):
+        for part in GROUPED[trip]:
+            for side in range(2):
+                side_copy(part, side).wait()
+        scale = 1.0 / count
 
         @pl.loop(0, rows // 8)
         def _(step):
             at = pl.ds(pl.multiple_of(step * 8, 8), 8)
-            tile = (summed[part][0, at, :] + beside[part][0, at, :] + beside[part][1, at, :]) / count
-            for half in range(8 // piece):
-                pieces[part][step * (8 // piece) + half] = tile[half * piece : (half + 1) * piece]
+            begin = 0
+            for part in GROUPED[trip]:
+                tile = (
+                    summed[part][0, at, :] + beside[part][0, at, :] + beside[part][1, at, :]
+                ) * scale
+                end = begin + tile.shape[1]
+                for half in range(8 // piece):
+                    pieces[trip][step * (8 // piece) + half, :, begin:end] = tile[
+                        half * piece : (half + 1) * piece
+                    ]
+                begin = end
 
         @pl.loop(1, groups)
         def _(step):
-            out_copy(part, place, rotated(place, step, groups)).start()
-        out_local(part).start()
-
-    for part in range(2):
+            out_copy(trip, place, rotated(place, step, groups)).start()
+        out_local(trip).start()
+
+    def send_back(part):
         out_local(part).wait()
 
         @pl.loop(1, groups)
@@ -346,6 +363,16 @@
             back_copy(part, place, rotated(place, step, groups)).start()
         back_local(part).start()
 
+    follow(1)
+    send_sides(0)
+    follow(2)
+    send_sides(1)
+    send_pieces(0)
+    send_sides(2)
+    send_pieces(1)
+    for trip in range(TRIPS):
+        send_back(trip)
+
     def turn_copy(turn):
         return pltpu.make_async_remote_copy(
             src_ref=block.at[turn], dst_ref=turned.at[turn - 1],
@@ -353,27 +380,27 @@
             device_id=(place, rotated(me, turn, TA)), device_id_type=MESH,
         )
 
-    for part in range(2):
-        low, high = PARTS[part]
-        back_local(part).wait()
+    for trip in range(TRIPS):
+        columns = [column for part in GROUPED[trip] for column in range(*PARTS[part])]
+        back_local(trip).wait()
 
         @pl.loop(1, groups)
         def _(step):
-            back_copy(part, rotated(place, groups - step, groups), place).wait_recv()
+            back_copy(trip, rotated(place, groups - step, groups), place).wait_recv()
 
         @pl.loop(0, rows // 8)
         def _(step):
             for half in range(8 // piece):
-                tile = owned[part][step * (8 // piece) + half]
-                for column in range(low, high):
+                tile = owned[trip][step * (8 // piece) + half]
+                for slot, column in enumerate(columns):
                     block[column, pl.ds(step * 8 + half * piece, piece), :] = tile[
-                        :, (column - low) * rows : (column - low + 1) * rows
+                        :, slot * rows : (slot + 1) * rows
                     ]
 
-        for column in range(low, high):
+        for column in columns:
             if 1 <= column <= turns:
                 turn_copy(column).start()
-        for column in range(low, high):
+        for column in columns:
             target = rotated(me, column, TA)
             out_ref[:, pl.ds(pl.multiple_of(target * rows, rows), rows)] = block[column]
 
@@ -385,16 +412,16 @@
     @pl.loop(1, TA)
     def _(step):
         target = rotated(me, step, TA)
-        gram_copy(1, me, target).wait_send()
+        gram_copy(COUNT - 1, me, target).wait_send()
         for chunk in range(CHUNKS - AHEAD, CHUNKS):
             line_copy(chunk, me, target).wait_send()
 
     @pl.loop(1, groups)
     def _(step):
         target = rotated(place, step, groups)
-        for part in range(2):
-            out_copy(part, place, target).wait_send()
-            back_copy(part, place, target).wait_send()
+        for trip in range(TRIPS):
+            out_copy(trip, place, target).wait_send()
+            back_copy(trip, place, target).wait_send()
 
 
 def on_device(field, weight, coef, window_start, window_end, owner_map):
@@ -408,8 +435,9 @@
     dma = pltpu.SemaphoreType.DMA
     turns = TA - KEPT
     widths = [(high - low) * rows for low, high in PARTS]
-
-    def part_scratch(*shape):
+    trips = [sum(widths[part] for part in parts) for parts in GROUPED]
+
+    def scratch(widths, *shape):
         return [pltpu.VMEM((*shape, width), jnp.float32) for width in widths]
 
     owned = pl.pallas_call(
@@ -429,24 +457,24 @@
             pltpu.VMEM((KEPT, rows, rows), jnp.float32),
             pltpu.VMEM((turns, rows, rows), jnp.float32),
             dma((CHUNKS, TA)), dma((CHUNKS, TA)), dma((CHUNKS,)),
-            dma((2, TA)), dma((2, TA)), dma((2,)),
-            dma((2, 2)), dma((2, 2)),
-            dma((2, groups)), dma((2, groups)), dma((2,)),
-            dma((2, groups)), dma((2, groups)), dma((2,)),
+            dma((COUNT, TA)), dma((COUNT, TA)), dma((COUNT,)),
+            dma((COUNT, 2)), dma((COUNT, 2)),
+            dma((TRIPS, groups)), dma((TRIPS, groups)), dma((TRIPS,)),
+            dma((TRIPS, groups)), dma((TRIPS, groups)), dma((TRIPS,)),
             dma((turns,)), dma((turns,)),
-            *part_scratch(TA, rows),
-            *part_scratch(3, rows),
-            *part_scratch(2, rows),
-            *part_scratch(groups, piece),
-            *part_scratch(groups, piece),
-            *part_scratch(groups, piece),
-            *part_scratch(groups, piece),
+            *scratch(widths, TA, rows),
+            *scratch(widths, 3, rows),
+            *scratch(widths, 2, rows),
+            *scratch(trips, groups, piece),
+            *scratch(trips, groups, piece),
+            *scratch(trips, groups, piece),
+            *scratch(trips, groups, piece),
         ],
         compiler_params=pltpu.CompilerParams(
             collective_id=0, has_side_effects=True, vmem_limit_bytes=48 * 1024 * 1024
         ),
         name="window_rows",
-    )(lines, weight[None], coef, window_start, window_end, owner_map)
+    )(lines, weight.reshape(WIDTH // 128, 128), coef, window_start, window_end, owner_map)
     return owned[None]
 
 

time: 120 us -> 116 us (0.967)
  Pallas kernels: 114 us -> 112 us
    pallas_call x1, Pallas kernels: 114 us -> 112 us  [on_device(): pl.pallas_call(functools.partial(window_kernel, rows, total, groups), out...]
    unnamed x10 -> x12, local copies, waits for them, and re-layouts: 3.56 us -> 3.57 us
where the time goes in v5:
time: 116 us; the launch traced here: 115 us
  Pallas kernels  112 us (97%)
  local copies, waits for them, and re-layouts  3.57 us (3%)
    pallas_call x1, Pallas kernels, on_device(): pl.pallas_call(functools.partial(window_kernel, rows, total, groups), out...  112 us
    unnamed x12, local copies, waits for them, and re-layouts  3.57 us

profile of v5, /device:TPU:2, one launch (start us, length us, event | category | flops | bytes accessed | tf_op | source)
XLA Modules:
  0.0 115.3 jit_solution(10830660221276872726)
XLA Ops:
  0.0 0.0 copy-start
  0.0 0.0 copy-start.1
  0.0 0.0 copy-start.2
  0.0 0.0 copy-start.3
  0.0 0.0 copy-start.4
  0.0 2.8 %copy.9 = bf16[128,8,1792]{2,0,1:T(8,128)(2,1)S(1)} copy(bf16[128,8,1792]{2,1,0:T(8,128)(2,1)} %param.6) | data formatting | bytes 7340032 | tf_op args[0]
  2.8 0.0 copy-done
  2.8 0.0 copy-done.1
  2.8 0.0 copy-done.2
  2.8 0.0 copy-done.3
  2.8 0.0 copy-done.4
  2.8 111.7 %window_rows.1 = f32[128,1024]{1,0:T(8,128)S(1)} custom-call(bf16[8,128,1792]{2,1,0:T(8,128)(2,1)S(1)} %bitcast.5, f32[14,128]{1,0:T(8,128)S(1)} %bitcast.7, f32[5,224]{1,0:T(8,128)S(1)} %copy-done.1, s32[32]{0:T(128)S(1)} %copy-done.2, s32[32]{0:T(128)S(1)} %copy-done.3, s32[32]{0:T(128)S(1)} %copy-done.4), custom_call_target="tpu_custom_call" | custom-call | tf_op jit(solution)/shard_map/window_rows/pallas_call | solution.py:443
  114.5 0.8 copy.11
Async XLA Ops:
  0.0 2.8 %copy-start = (f32[1792]{0:T(1024)S(1)}, f32[1792]{0:T(1024)}, u32[]{:S(2)}) copy-start(f32[1792]{0:T(1024)} %param.7) | copy-start | bytes 21508
  0.0 2.8 %copy-start.1 = (f32[5,224]{1,0:T(8,128)S(1)}, f32[5,224]{1,0:T(8,128)}, u32[]{:S(2)}) copy-start(f32[5,224]{1,0:T(8,128)} %coef_ref.1) | copy-start | bytes 13444
  0.0 2.8 %copy-start.2 = (s32[32]{0:T(128)S(1)}, s32[32]{0:T(128)}, u32[]{:S(2)}) copy-start(s32[32]{0:T(128)} %start_ref.1) | copy-start | bytes 388
  0.0 2.8 %copy-start.3 = (s32[32]{0:T(128)S(1)}, s32[32]{0:T(128)}, u32[]{:S(2)}) copy-start(s32[32]{0:T(128)} %end_ref.1) | copy-start | bytes 388
  0.0 2.8 %copy-start.4 = (s32[32]{0:T(128)S(1)}, s32[32]{0:T(128)}, u32[]{:S(2)}) copy-start(s32[32]{0:T(128)} %owner_ref.1) | copy-start | bytes 388

commit v6 on v5

--- a/solution.py
+++ b/solution.py
@@ -295,8 +295,22 @@
     def out_copy(part, owner, target):
         return pltpu.make_async_remote_copy(
             src_ref=pieces[part].at[target], dst_ref=spread[part].at[owner],
-            send_sem=out_send.at[part, target], recv_sem=out_recv.at[part, owner],
+            send_sem=out_send.at[part], recv_sem=out_recv.at[part],
             device_id=(target, me), device_id_type=MESH,
+        )
+
+    def out_all(part):
+        return pltpu.make_async_remote_copy(
+            src_ref=pieces[part].at[: groups - 1], dst_ref=spread[part].at[: groups - 1],
+            send_sem=out_send.at[part], recv_sem=out_recv.at[part],
+            device_id=(place, me), device_id_type=MESH,
+        )
+
+    def back_all(part):
+        return pltpu.make_async_remote_copy(
+            src_ref=ordered[part].at[: groups - 1], dst_ref=owned[part].at[: groups - 1],
+            send_sem=back_send.at[part], recv_sem=back_recv.at[part],
+            device_id=(place, me), device_id_type=MESH,
         )
 
     def out_local(part):
@@ -307,7 +321,7 @@
     def back_copy(part, owner, target):
         return pltpu.make_async_remote_copy(
             src_ref=ordered[part].at[target], dst_ref=owned[part].at[owner],
-            send_sem=back_send.at[part, target], recv_sem=back_recv.at[part, owner],
+            send_sem=back_send.at[part], recv_sem=back_recv.at[part],
             device_id=(target, me), device_id_type=MESH,
         )
 
@@ -350,9 +364,7 @@
     def send_back(part):
         out_local(part).wait()
 
-        @pl.loop(1, groups)
-        def _(step):
-            out_copy(part, rotated(place, groups - step, groups), place).wait_recv()
+        out_all(part).wait_recv()
 
         @pl.loop(0, groups)
         def _(slot):
@@ -380,13 +392,22 @@
             device_id=(place, rotated(me, turn, TA)), device_id_type=MESH,
         )
 
+    @pl.loop(1, TA)
+    def _(step):
+        target = rotated(me, step, TA)
+        gram_copy(COUNT - 1, me, target).wait_send()
+        for chunk in range(CHUNKS - AHEAD, CHUNKS):
+            line_copy(chunk, me, target).wait_send()
+
+    for trip in range(TRIPS):
+        out_all(trip).wait_send()
+        back_all(trip).wait_send()
+
     for trip in range(TRIPS):
         columns = [column for part in GROUPED[trip] for column in range(*PARTS[part])]
         back_local(trip).wait()
 
-        @pl.loop(1, groups)
-        def _(step):
-            back_copy(trip, rotated(place, groups - step, groups), place).wait_recv()
+        back_all(trip).wait_recv()
 
         @pl.loop(0, rows // 8)
         def _(step):
@@ -408,20 +429,6 @@
         turn_copy(turn).wait()
         target = rotated(me, TA - turn, TA)
         out_ref[:, pl.ds(pl.multiple_of(target * rows, rows), rows)] = turned[turn - 1].T
-
-    @pl.loop(1, TA)
-    def _(step):
-        target = rotated(me, step, TA)
-        gram_copy(COUNT - 1, me, target).wait_send()
-        for chunk in range(CHUNKS - AHEAD, CHUNKS):
-            line_copy(chunk, me, target).wait_send()
-
-    @pl.loop(1, groups)
-    def _(step):
-        target = rotated(place, step, groups)
-        for trip in range(TRIPS):
-            out_copy(trip, place, target).wait_send()
-            back_copy(trip, place, target).wait_send()
 
 
 def on_device(field, weight, coef, window_start, window_end, owner_map):
@@ -459,8 +466,8 @@
             dma((CHUNKS, TA)), dma((CHUNKS, TA)), dma((CHUNKS,)),
             dma((COUNT, TA)), dma((COUNT, TA)), dma((COUNT,)),
             dma((COUNT, 2)), dma((COUNT, 2)),
-            dma((TRIPS, groups)), dma((TRIPS, groups)), dma((TRIPS,)),
-            dma((TRIPS, groups)), dma((TRIPS, groups)), dma((TRIPS,)),
+            dma((TRIPS,)), dma((TRIPS,)), dma((TRIPS,)),
+            dma((TRIPS,)), dma((TRIPS,)), dma((TRIPS,)),
             dma((turns,)), dma((turns,)),
             *scratch(widths, TA, rows),
             *scratch(widths, 3, rows),

time: 116 us -> 113 us (0.974)
  Pallas kernels: 112 us -> 109 us
    pallas_call x1, Pallas kernels: 112 us -> 109 us  [on_device(): pl.pallas_call(functools.partial(window_kernel, rows, total, groups), out...]
where the time goes in v6:
time: 113 us; the launch traced here: 112 us
  Pallas kernels  109 us (96%)
  local copies, waits for them, and re-layouts  3.57 us (3%)
    pallas_call x1, Pallas kernels, on_device(): pl.pallas_call(functools.partial(window_kernel, rows, total, groups), out...  109 us
    unnamed x12, local copies, waits for them, and re-layouts  3.57 us

profile of v6, /device:TPU:2, one launch (start us, length us, event | category | flops | bytes accessed | tf_op | source)
XLA Modules:
  0.0 112.2 jit_solution(8993133221266557176)
XLA Ops:
  0.0 0.0 copy-start
  0.0 0.0 copy-start.1
  0.0 0.0 copy-start.2
  0.0 0.0 copy-start.3
  0.0 0.0 copy-start.4
  0.0 2.8 %copy.9 = bf16[128,8,1792]{2,0,1:T(8,128)(2,1)S(1)} copy(bf16[128,8,1792]{2,1,0:T(8,128)(2,1)} %param.6) | data formatting | bytes 7340032 | tf_op args[0]
  2.8 0.0 copy-done
  2.8 0.0 copy-done.1
  2.8 0.0 copy-done.2
  2.8 0.0 copy-done.3
  2.8 0.0 copy-done.4
  2.8 108.5 %window_rows.1 = f32[128,1024]{1,0:T(8,128)S(1)} custom-call(bf16[8,128,1792]{2,1,0:T(8,128)(2,1)S(1)} %bitcast.5, f32[14,128]{1,0:T(8,128)S(1)} %bitcast.7, f32[5,224]{1,0:T(8,128)S(1)} %copy-done.1, s32[32]{0:T(128)S(1)} %copy-done.2, s32[32]{0:T(128)S(1)} %copy-done.3, s32[32]{0:T(128)S(1)} %copy-done.4), custom_call_target="tpu_custom_call" | custom-call | tf_op jit(solution)/shard_map/window_rows/pallas_call | solution.py:450
  111.4 0.8 copy.11
Async XLA Ops:
  0.0 2.8 %copy-start = (f32[1792]{0:T(1024)S(1)}, f32[1792]{0:T(1024)}, u32[]{:S(2)}) copy-start(f32[1792]{0:T(1024)} %param.7) | copy-start | bytes 21508
  0.0 2.8 %copy-start.1 = (f32[5,224]{1,0:T(8,128)S(1)}, f32[5,224]{1,0:T(8,128)}, u32[]{:S(2)}) copy-start(f32[5,224]{1,0:T(8,128)} %coef_ref.1) | copy-start | bytes 13444
  0.0 2.8 %copy-start.2 = (s32[32]{0:T(128)S(1)}, s32[32]{0:T(128)}, u32[]{:S(2)}) copy-start(s32[32]{0:T(128)} %start_ref.1) | copy-start | bytes 388
  0.0 2.8 %copy-start.3 = (s32[32]{0:T(128)S(1)}, s32[32]{0:T(128)}, u32[]{:S(2)}) copy-start(s32[32]{0:T(128)} %end_ref.1) | copy-start | bytes 388
  0.0 2.8 %copy-start.4 = (s32[32]{0:T(128)S(1)}, s32[32]{0:T(128)}, u32[]{:S(2)}) copy-start(s32[32]{0:T(128)} %owner_ref.1) | copy-start | bytes 388

commit v7 on v6

--- a/solution.py
+++ b/solution.py
@@ -69,8 +69,17 @@
         return pltpu.make_async_remote_copy(
             src_ref=send.at[target, :, lanes],
             dst_ref=lines.at[pl.ds(pl.multiple_of(owner * rows, rows), rows), lanes],
-            send_sem=line_send.at[chunk, target], recv_sem=line_recv.at[chunk, owner],
+            send_sem=line_send.at[chunk], recv_sem=line_recv.at[chunk],
             device_id=(place, target), device_id_type=MESH,
+        )
+
+    def all_lines(chunk):
+        lanes = slice(CUTS[chunk], CUTS[chunk + 1])
+        some = lines.at[: (TA - 1) * rows, lanes]
+        return pltpu.make_async_remote_copy(
+            src_ref=some, dst_ref=some,
+            send_sem=line_send.at[chunk], recv_sem=line_recv.at[chunk],
+            device_id=(place, me), device_id_type=MESH,
         )
 
     def own_copy(chunk):
@@ -150,15 +159,10 @@
     for chunk in range(CHUNKS):
         own_copy(chunk).wait()
 
-        @pl.loop(1, TA)
-        def _(step):
-            line_copy(chunk, rotated(me, step, TA), me).wait_recv()
+        all_lines(chunk).wait_recv()
 
         if chunk + AHEAD < CHUNKS:
-
-            @pl.loop(1, TA)
-            def _(step):
-                line_copy(chunk, me, rotated(me, step, TA)).wait_send()
+            all_lines(chunk).wait_send()
             start_lines(chunk + AHEAD)
 
         new = slice(CUTS[chunk], CUTS[chunk + 1])
@@ -168,7 +172,7 @@
             start = pl.multiple_of(step * 16, 16)
             tile = lines[pl.ds(start, 16), new].astype(jnp.float32)
             return acc + tile
-        acc = lax.fori_loop(0, total // 16, add, jnp.zeros((16, fresh), jnp.float32))
+        acc = lax.fori_loop(0, total // 16, add, jnp.zeros((16, fresh), jnp.float32), unroll=4)
         mean[:, new] = jnp.sum(acc, axis=0, keepdims=True) * (1.0 / total)
 
         first, last = DONE[chunk], DONE[chunk + 1]
@@ -396,9 +400,9 @@
     def _(step):
         target = rotated(me, step, TA)
         gram_copy(COUNT - 1, me, target).wait_send()
-        for chunk in range(CHUNKS - AHEAD, CHUNKS):
-            line_copy(chunk, me, target).wait_send()
-
+
+    for chunk in range(CHUNKS - AHEAD, CHUNKS):
+        all_lines(chunk).wait_send()
     for trip in range(TRIPS):
         out_all(trip).wait_send()
         back_all(trip).wait_send()
@@ -424,11 +428,11 @@
         for column in columns:
             target = rotated(me, column, TA)
             out_ref[:, pl.ds(pl.multiple_of(target * rows, rows), rows)] = block[column]
-
-    for turn in range(1, turns + 1):
-        turn_copy(turn).wait()
-        target = rotated(me, TA - turn, TA)
-        out_ref[:, pl.ds(pl.multiple_of(target * rows, rows), rows)] = turned[turn - 1].T
+        if trip == 0:
+            for turn in range(1, turns + 1):
+                turn_copy(turn).wait()
+                target = rotated(me, TA - turn, TA)
+                out_ref[:, pl.ds(pl.multiple_of(target * rows, rows), rows)] = turned[turn - 1].T
 
 
 def on_device(field, weight, coef, window_start, window_end, owner_map):
@@ -463,7 +467,7 @@
             pltpu.VMEM((total, PAIR * rows), jnp.float32),
             pltpu.VMEM((KEPT, rows, rows), jnp.float32),
             pltpu.VMEM((turns, rows, rows), jnp.float32),
-            dma((CHUNKS, TA)), dma((CHUNKS, TA)), dma((CHUNKS,)),
+            dma((CHUNKS,)), dma((CHUNKS,)), dma((CHUNKS,)),
             dma((COUNT, TA)), dma((COUNT, TA)), dma((COUNT,)),
             dma((COUNT, 2)), dma((COUNT, 2)),
             dma((TRIPS,)), dma((TRIPS,)), dma((TRIPS,)),

time: 113 us -> 112 us (level)
  no operation moved by 1% of the time
where the time goes in v7:
time: 112 us; the launch traced here: 111 us
  Pallas kernels  108 us (96%)
  local copies, waits for them, and re-layouts  3.57 us (3%)
    pallas_call x1, Pallas kernels, on_device(): pl.pallas_call(functools.partial(window_kernel, rows, total, groups), out...  108 us
    unnamed x12, local copies, waits for them, and re-layouts  3.57 us

profile of v7, /device:TPU:2, one launch (start us, length us, event | category | flops | bytes accessed | tf_op | source)
XLA Modules:
  0.0 111.2 jit_solution(11612103328230018142)
XLA Ops:
  0.0 0.0 copy-start
  0.0 0.0 copy-start.1
  0.0 0.0 copy-start.2
  0.0 0.0 copy-start.3
  0.0 0.0 copy-start.4
  0.0 2.8 %copy.9 = bf16[128,8,1792]{2,0,1:T(8,128)(2,1)S(1)} copy(bf16[128,8,1792]{2,1,0:T(8,128)(2,1)} %param.6) | data formatting | bytes 7340032 | tf_op args[0]
  2.8 0.0 copy-done
  2.8 0.0 copy-done.1
  2.8 0.0 copy-done.2
  2.8 0.0 copy-done.3
  2.8 0.0 copy-done.4
  2.8 107.5 %window_rows.1 = f32[128,1024]{1,0:T(8,128)S(1)} custom-call(bf16[8,128,1792]{2,1,0:T(8,128)(2,1)S(1)} %bitcast.5, f32[14,128]{1,0:T(8,128)S(1)} %bitcast.7, f32[5,224]{1,0:T(8,128)S(1)} %copy-done.1, s32[32]{0:T(128)S(1)} %copy-done.2, s32[32]{0:T(128)S(1)} %copy-done.3, s32[32]{0:T(128)S(1)} %copy-done.4), custom_call_target="tpu_custom_call" | custom-call | tf_op jit(solution)/shard_map/window_rows/pallas_call | solution.py:454
  110.4 0.8 copy.11
Async XLA Ops:
  0.0 2.8 %copy-start = (f32[1792]{0:T(1024)S(1)}, f32[1792]{0:T(1024)}, u32[]{:S(2)}) copy-start(f32[1792]{0:T(1024)} %param.7) | copy-start | bytes 21508
  0.0 2.8 %copy-start.1 = (f32[5,224]{1,0:T(8,128)S(1)}, f32[5,224]{1,0:T(8,128)}, u32[]{:S(2)}) copy-start(f32[5,224]{1,0:T(8,128)} %coef_ref.1) | copy-start | bytes 13444
  0.0 2.8 %copy-start.2 = (s32[32]{0:T(128)S(1)}, s32[32]{0:T(128)}, u32[]{:S(2)}) copy-start(s32[32]{0:T(128)} %start_ref.1) | copy-start | bytes 388
  0.0 2.8 %copy-start.3 = (s32[32]{0:T(128)S(1)}, s32[32]{0:T(128)}, u32[]{:S(2)}) copy-start(s32[32]{0:T(128)} %end_ref.1) | copy-start | bytes 388
  0.0 2.8 %copy-start.4 = (s32[32]{0:T(128)S(1)}, s32[32]{0:T(128)}, u32[]{:S(2)}) copy-start(s32[32]{0:T(128)} %owner_ref.1) | copy-start | bytes 388

commit v8 on v7

--- a/solution.py
+++ b/solution.py
@@ -115,11 +115,11 @@
         own_copy(chunk).start()
 
     for tile in range(WIDTH // 128):
-        base[:, 128 * tile : 128 * (tile + 1)] = weight_ref[tile : tile + 1, :]
+        base[:1, 128 * tile : 128 * (tile + 1)] = weight_ref[tile : tile + 1, :]
     weight = jnp.zeros((1, NYW), jnp.float32)
     for station in range(STATIONS):
         weight = jnp.where(
-            me == station, base[:, NYW * station : NYW * (station + 1)], weight
+            me == station, base[:1, NYW * station : NYW * (station + 1)], weight
         )
     reach = (
         lax.broadcasted_iota(jnp.int32, (2 * BAND + 1, NYW), 1)
@@ -182,22 +182,20 @@
 
         middle = slice(first - low, last - low)
         level = mean[:, low:high]
-        offset_level = jnp.zeros((1, last - first), jnp.float32)
         for offset in range(2 * BAND + 1):
             moved = level if offset == BAND else pltpu.roll(level, (BAND - offset) % (high - low), 1)
-            offset_level = offset_level + taps[offset : offset + 1, lanes] * moved[:, middle]
-        base[:, lanes] = offset_level
+            base[offset : offset + 1, lanes] = moved[:, middle]
 
         @pl.loop(0, total // tall)
         def _(step):
             at = pl.ds(pl.multiple_of(step * tall, tall), tall)
             raw = lines[at, low:high]
-            filtered = taps[BAND : BAND + 1, lanes] * raw[:, middle].astype(jnp.float32)
+            filtered = jnp.zeros((tall, last - first), jnp.float32)
             for offset in range(2 * BAND + 1):
-                if offset != BAND:
-                    moved = pltpu.roll(raw, (BAND - offset) % (high - low), 1)[:, middle]
-                    filtered = filtered + taps[offset : offset + 1, lanes] * moved.astype(jnp.float32)
-            scaled[at, lanes] = (filtered - base[:, lanes]).astype(jnp.bfloat16)
+                moved = raw if offset == BAND else pltpu.roll(raw, (BAND - offset) % (high - low), 1)
+                centered = moved[:, middle].astype(jnp.float32) - base[offset : offset + 1, lanes]
+                filtered = filtered + taps[offset : offset + 1, lanes] * centered
+            scaled[at, lanes] = filtered.astype(jnp.bfloat16)
 
         def multiply(row, blocks):
             where = pl.ds(pl.multiple_of(row * pair, pair), pair)
@@ -463,7 +461,7 @@
             pltpu.VMEM((total, WIDTH), jnp.bfloat16),
             pltpu.VMEM((2 * BAND + 1, WIDTH), jnp.float32),
             pltpu.VMEM((1, WIDTH), jnp.float32),
-            pltpu.VMEM((1, WIDTH), jnp.float32),
+            pltpu.VMEM((2 * BAND + 1, WIDTH), jnp.float32),
             pltpu.VMEM((total, PAIR * rows), jnp.float32),
             pltpu.VMEM((KEPT, rows, rows), jnp.float32),
             pltpu.VMEM((turns, rows, rows), jnp.float32),

time: 112 us -> 112 us (level)
  no operation moved by 1% of the time
where the time goes in v8:
time: 112 us; the launch traced here: 111 us
  Pallas kernels  108 us (96%)
  local copies, waits for them, and re-layouts  3.57 us (3%)
    pallas_call x1, Pallas kernels, on_device(): pl.pallas_call(functools.partial(window_kernel, rows, total, groups), out...  108 us
    unnamed x12, local copies, waits for them, and re-layouts  3.57 us

profile of v8, /device:TPU:2, one launch (start us, length us, event | category | flops | bytes accessed | tf_op | source)
XLA Modules:
  0.0 111.3 jit_solution(1295755314214483072)
XLA Ops:
  0.0 0.0 copy-start
  0.0 0.0 copy-start.1
  0.0 0.0 copy-start.2
  0.0 0.0 copy-start.3
  0.0 0.0 copy-start.4
  0.0 2.8 %copy.9 = bf16[128,8,1792]{2,0,1:T(8,128)(2,1)S(1)} copy(bf16[128,8,1792]{2,1,0:T(8,128)(2,1)} %param.6) | data formatting | bytes 7340032 | tf_op args[0]
  2.8 0.0 copy-done
  2.8 0.0 copy-done.1
  2.8 0.0 copy-done.2
  2.8 0.0 copy-done.3
  2.8 0.0 copy-done.4
  2.8 107.6 %window_rows.1 = f32[128,1024]{1,0:T(8,128)S(1)} custom-call(bf16[8,128,1792]{2,1,0:T(8,128)(2,1)S(1)} %bitcast.5, f32[14,128]{1,0:T(8,128)S(1)} %bitcast.7, f32[5,224]{1,0:T(8,128)S(1)} %copy-done.1, s32[32]{0:T(128)S(1)} %copy-done.2, s32[32]{0:T(128)S(1)} %copy-done.3, s32[32]{0:T(128)S(1)} %copy-done.4), custom_call_target="tpu_custom_call" | custom-call | tf_op jit(solution)/shard_map/window_rows/pallas_call | solution.py:452
  110.5 0.8 copy.11
Async XLA Ops:
  0.0 2.8 %copy-start = (f32[1792]{0:T(1024)S(1)}, f32[1792]{0:T(1024)}, u32[]{:S(2)}) copy-start(f32[1792]{0:T(1024)} %param.7) | copy-start | bytes 21508
  0.0 2.8 %copy-start.1 = (f32[5,224]{1,0:T(8,128)S(1)}, f32[5,224]{1,0:T(8,128)}, u32[]{:S(2)}) copy-start(f32[5,224]{1,0:T(8,128)} %coef_ref.1) | copy-start | bytes 13444
  0.0 2.8 %copy-start.2 = (s32[32]{0:T(128)S(1)}, s32[32]{0:T(128)}, u32[]{:S(2)}) copy-start(s32[32]{0:T(128)} %start_ref.1) | copy-start | bytes 388
  0.0 2.8 %copy-start.3 = (s32[32]{0:T(128)S(1)}, s32[32]{0:T(128)}, u32[]{:S(2)}) copy-start(s32[32]{0:T(128)} %end_ref.1) | copy-start | bytes 388
  0.0 2.8 %copy-start.4 = (s32[32]{0:T(128)S(1)}, s32[32]{0:T(128)}, u32[]{:S(2)}) copy-start(s32[32]{0:T(128)} %owner_ref.1) | copy-start | bytes 388

commit v9 on v8

--- a/solution.py
+++ b/solution.py
@@ -58,7 +58,7 @@
             barrier, inc=1, device_id=(place, rotated(me, step, TA)), device_id_type=MESH
         )
 
-    @pl.loop(1, groups)
+    @pl.loop(1, groups, unroll=True)
     def _(step):
         pl.semaphore_signal(
             barrier, inc=1, device_id=(rotated(place, step, groups), me), device_id_type=MESH
@@ -358,7 +358,7 @@
                     ]
                 begin = end
 
-        @pl.loop(1, groups)
+        @pl.loop(1, groups, unroll=True)
         def _(step):
             out_copy(trip, place, rotated(place, step, groups)).start()
         out_local(trip).start()
@@ -372,7 +372,7 @@
         def _(slot):
             ordered[part][slot] = spread[part][source[slot]]
 
-        @pl.loop(1, groups)
+        @pl.loop(1, groups, unroll=True)
         def _(step):
             back_copy(part, place, rotated(place, step, groups)).start()
         back_local(part).start()

time: 112 us -> 112 us (level)
  no operation moved by 1% of the time
where the time goes in v9:
time: 112 us; the launch traced here: 111 us
  Pallas kernels  107 us (96%)
  local copies, waits for them, and re-layouts  3.57 us (3%)
    pallas_call x1, Pallas kernels, on_device(): pl.pallas_call(functools.partial(window_kernel, rows, total, groups), out...  107 us
    unnamed x12, local copies, waits for them, and re-layouts  3.57 us

profile of v9, /device:TPU:2, one launch (start us, length us, event | category | flops | bytes accessed | tf_op | source)
XLA Modules:
  0.0 111.1 jit_solution(732471620635827588)
XLA Ops:
  0.0 0.0 copy-start
  0.0 0.0 copy-start.1
  0.0 0.0 copy-start.2
  0.0 0.0 copy-start.3
  0.0 0.0 copy-start.4
  0.0 2.8 %copy.9 = bf16[128,8,1792]{2,0,1:T(8,128)(2,1)S(1)} copy(bf16[128,8,1792]{2,1,0:T(8,128)(2,1)} %param.6) | data formatting | bytes 7340032 | tf_op args[0]
  2.8 0.0 copy-done
  2.8 0.0 copy-done.1
  2.8 0.0 copy-done.2
  2.8 0.0 copy-done.3
  2.8 0.0 copy-done.4
  2.8 107.5 %window_rows.1 = f32[128,1024]{1,0:T(8,128)S(1)} custom-call(bf16[8,128,1792]{2,1,0:T(8,128)(2,1)S(1)} %bitcast.5, f32[14,128]{1,0:T(8,128)S(1)} %bitcast.7, f32[5,224]{1,0:T(8,128)S(1)} %copy-done.1, s32[32]{0:T(128)S(1)} %copy-done.2, s32[32]{0:T(128)S(1)} %copy-done.3, s32[32]{0:T(128)S(1)} %copy-done.4), custom_call_target="tpu_custom_call" | custom-call | tf_op jit(solution)/shard_map/window_rows/pallas_call | solution.py:452
  110.3 0.8 copy.11
Async XLA Ops:
  0.0 2.8 %copy-start = (f32[1792]{0:T(1024)S(1)}, f32[1792]{0:T(1024)}, u32[]{:S(2)}) copy-start(f32[1792]{0:T(1024)} %param.7) | copy-start | bytes 21508
  0.0 2.8 %copy-start.1 = (f32[5,224]{1,0:T(8,128)S(1)}, f32[5,224]{1,0:T(8,128)}, u32[]{:S(2)}) copy-start(f32[5,224]{1,0:T(8,128)} %coef_ref.1) | copy-start | bytes 13444
  0.0 2.8 %copy-start.2 = (s32[32]{0:T(128)S(1)}, s32[32]{0:T(128)}, u32[]{:S(2)}) copy-start(s32[32]{0:T(128)} %start_ref.1) | copy-start | bytes 388
  0.0 2.8 %copy-start.3 = (s32[32]{0:T(128)S(1)}, s32[32]{0:T(128)}, u32[]{:S(2)}) copy-start(s32[32]{0:T(128)} %end_ref.1) | copy-start | bytes 388
  0.0 2.8 %copy-start.4 = (s32[32]{0:T(128)S(1)}, s32[32]{0:T(128)}, u32[]{:S(2)}) copy-start(s32[32]{0:T(128)} %owner_ref.1) | copy-start | bytes 388
